TPU v7x, 32 devices: a whole 2x2x4 slice. The times are simulated.
32 devices in a mesh: dp: 16 (over z, y, x), tensor: 2 (over core).
Axes of the slice: x: 2, y: 2, z: 4, core: 2. Of those that a mesh axis runs over, the one named last changes fastest.
Arguments:
- queries: bfloat16 [16384, 3072], P('dp', 'tensor'), may hold values from -70 to 70
- keys: bfloat16 [16384, 3072], P('dp', 'tensor'), may hold values from -5 to 5
- values: bfloat16 [16384, 3072], P('dp', 'tensor'), may hold values from -6 to 6
- out_gradient: bfloat16 [16384, 5120], P(('dp', 'tensor')), may hold values from -6 to 6
- out_weight: bfloat16 [3072, 5120], P('tensor'), may hold values from -0.109375 to 0.109375
- segments: int32 [16, 8], replicated, may hold values from 0 to 7, as said below
- counts: int32 [16], replicated, may hold values from 1 to 4, as said below
Outputs:
- query_gradient: bfloat16 [16384, 3072], P('dp', 'tensor')
- key_gradient: bfloat16 [16384, 3072], P('dp', 'tensor')
- value_gradient: bfloat16 [16384, 3072], P('dp', 'tensor')
- weight_gradient: float32 [5120, 3072], P('dp', 'tensor')
Inputs may be any that keep to these rules, and one draw needn't show every extreme that they name: `segments`: along each row ids never fall; each protein spans 1 to 4 consecutive blocks, and some protein spans exactly 4; the last counts[r] blocks of replica r are whole proteins. counts[r] equals counts[(r + 8) mod 16].
All inputs are finite; a program needn't handle non-finite values.
Results may differ from a plain program's by a relative error of at most 0.025.
Values may be sent and summed in bfloat16 or wider, within the bound.
A program may use at most 192 MiB of HBM per device.

v0:
```python
import jax
import jax.numpy as jnp
from jax import lax
from jax.sharding import PartitionSpec as P

HEAD_SIZE = 128
BLOCK = 128


masked_score = -1e30


def swapped(x, axis, distance):
    return lax.ppermute(x, axis, [(i, i ^ 1 << distance) for i in range(lax.axis_size(axis))])


def attend(query, key_rows, value, gradient, block_ids):
    length, inner = query.shape
    heads = inner // HEAD_SIZE
    scale = HEAD_SIZE ** (-0.5)
    total_blocks = block_ids.shape[0]
    window = total_blocks // 2

    def split(array, rows):
        return array.reshape(rows, heads, HEAD_SIZE)

    def visit(carry, index):
        key_total, value_total = carry
        own = block_ids[index]
        first = jnp.argmax(block_ids == own)
        start = jnp.minimum(first, total_blocks - window)
        query_block = split(lax.dynamic_slice_in_dim(query, index * BLOCK, BLOCK, 0), BLOCK)
        grad_block = split(lax.dynamic_slice_in_dim(gradient, index * BLOCK, BLOCK, 0), BLOCK)
        window_ids = lax.dynamic_slice_in_dim(block_ids, start, window, 0)
        key_window = split(
            lax.dynamic_slice_in_dim(key_rows, start * BLOCK, window * BLOCK, 0), window * BLOCK
        )
        value_window = split(
            lax.dynamic_slice_in_dim(value, start * BLOCK, window * BLOCK, 0), window * BLOCK
        )
        score_tiles = []
        grad_tiles = []
        for tile in range(window):
            key_tile = key_window[tile * BLOCK : (tile + 1) * BLOCK]
            value_tile = value_window[tile * BLOCK : (tile + 1) * BLOCK]

            def near(key_tile=key_tile, value_tile=value_tile):
                return (
                    jnp.einsum(
                        "qhd,khd->hqk", query_block, key_tile, preferred_element_type=jnp.float32
                    )
                    * scale,
                    jnp.einsum(
                        "qhd,khd->hqk", grad_block, value_tile, preferred_element_type=jnp.float32
                    ),
                )

            def far():
                return (
                    jnp.full((heads, BLOCK, BLOCK), masked_score, jnp.float32),
                    jnp.zeros((heads, BLOCK, BLOCK), jnp.float32),
                )

            score_tile, grad_tile = lax.cond(window_ids[tile] == own, near, far)
            score_tiles.append(score_tile)
            grad_tiles.append(grad_tile)
        scores = jnp.concatenate(score_tiles, axis=2)
        chance_gradient = jnp.concatenate(grad_tiles, axis=2)
        highest = jnp.max(scores, axis=2, keepdims=True)
        weights = jnp.exp(scores - highest)
        chances = weights / jnp.sum(weights, axis=2, keepdims=True)
        chance_weights = chances.astype(jnp.bfloat16)
        output_sum = jnp.zeros((BLOCK, heads, HEAD_SIZE), jnp.float32)
        for tile in range(window):
            value_tile = value_window[tile * BLOCK : (tile + 1) * BLOCK]
            weight_tile = chance_weights[:, :, tile * BLOCK : (tile + 1) * BLOCK]
            output_sum = output_sum + lax.cond(
                window_ids[tile] == own,
                lambda weight_tile=weight_tile, value_tile=value_tile: jnp.einsum(
                    "hqk,khd->qhd", weight_tile, value_tile, preferred_element_type=jnp.float32
                ),
                lambda: jnp.zeros((BLOCK, heads, HEAD_SIZE), jnp.float32),
            )
        head_output = output_sum.astype(jnp.bfloat16)
        centering = jnp.sum(
            grad_block.astype(jnp.float32) * head_output.astype(jnp.float32), axis=2
        )
        score_gradient = (
            chances * (chance_gradient - jnp.transpose(centering)[:, :, None])
        ).astype(jnp.bfloat16)
        query_sum = jnp.zeros((BLOCK, heads, HEAD_SIZE), jnp.float32)
        key_pieces = []
        value_pieces = []
        for tile in range(window):
            key_tile = key_window[tile * BLOCK : (tile + 1) * BLOCK]
            slope_tile = score_gradient[:, :, tile * BLOCK : (tile + 1) * BLOCK]
            weight_tile = chance_weights[:, :, tile * BLOCK : (tile + 1) * BLOCK]

            def near_back(key_tile=key_tile, slope_tile=slope_tile, weight_tile=weight_tile):
                return (
                    jnp.einsum(
                        "hqk,khd->qhd", slope_tile, key_tile, preferred_element_type=jnp.float32
                    ),
                    jnp.einsum(
                        "hqk,qhd->khd", slope_tile, query_block, preferred_element_type=jnp.float32
                    ),
                    jnp.einsum(
                        "hqk,qhd->khd", weight_tile, grad_block, preferred_element_type=jnp.float32
                    ),
                )

            def far_back():
                empty = jnp.zeros((BLOCK, heads, HEAD_SIZE), jnp.float32)
                return (empty, empty, empty)

            query_part, key_part, value_part = lax.cond(
                window_ids[tile] == own, near_back, far_back
            )
            query_sum = query_sum + query_part
            key_pieces.append(key_part.reshape(BLOCK, inner))
            value_pieces.append(value_part.reshape(BLOCK, inner))
        key_window_sum = jnp.concatenate(key_pieces, axis=0)
        value_window_sum = jnp.concatenate(value_pieces, axis=0)
        key_total = lax.dynamic_update_slice_in_dim(
            key_total,
            lax.dynamic_slice_in_dim(key_total, start * BLOCK, window * BLOCK, 0) + key_window_sum,
            start * BLOCK,
            0,
        )
        value_total = lax.dynamic_update_slice_in_dim(
            value_total,
            lax.dynamic_slice_in_dim(value_total, start * BLOCK, window * BLOCK, 0)
            + value_window_sum,
            start * BLOCK,
            0,
        )
        query_block_grad = (query_sum * scale).astype(jnp.bfloat16).reshape(BLOCK, inner)
        return ((key_total, value_total), (query_block_grad, head_output.reshape(BLOCK, inner)))

    start_totals = (
        jnp.zeros((length, inner), jnp.float32),
        jnp.zeros((length, inner), jnp.float32),
    )
    totals, stacked = lax.scan(visit, start_totals, jnp.arange(total_blocks, dtype=jnp.int32))
    query_local = stacked[0].reshape(length, inner)
    head_output = stacked[1].reshape(length, inner)
    key_local = (totals[0] * scale).astype(jnp.bfloat16)
    value_local = totals[1].astype(jnp.bfloat16)
    return (query_local, key_local, value_local, head_output)


def shards(queries, keys, values, out_gradient, out_weight, segments, counts):
    full_gradient = lax.all_gather(out_gradient, "tensor", axis=0, tiled=True)
    head_gradient = lax.dot_general(
        full_gradient, out_weight, (((1,), (1,)), ((), ())), preferred_element_type=jnp.float32
    ).astype(jnp.bfloat16)
    replicas = lax.axis_size("dp")
    halfway = replicas // 2
    position = lax.axis_index("dp")
    blocks = segments.shape[1]
    block_rows = queries.shape[0] // blocks
    trailing = blocks // 2 * block_rows
    moving = lax.dynamic_index_in_dim(counts, position, 0, keepdims=False)
    own_blocks = lax.dynamic_index_in_dim(segments, position, 0, keepdims=False)
    block_moved = jnp.arange(blocks, dtype=jnp.int32) >= blocks - moving
    row_moved = jnp.repeat(block_moved, block_rows)[-trailing:, None]
    flip_bit = halfway.bit_length() - 1

    def settle(local, arrived):
        upper = jnp.where(row_moved, arrived, local[-trailing:])
        return jnp.concatenate([local[:-trailing], upper], axis=0)

    query_local, key_local, value_local, head_output = attend(
        queries, keys, values, head_gradient, own_blocks
    )
    arrived = swapped(
        (query_local[-trailing:], key_local[-trailing:], value_local[-trailing:]), "dp", flip_bit
    )
    query_gradient = settle(query_local, arrived[0])
    key_gradient = settle(key_local, arrived[1])
    value_gradient = settle(value_local, arrived[2])
    weight_gradient = lax.psum_scatter(
        lax.dot_general(
            full_gradient, head_output, (((0,), (0,)), ((), ())), preferred_element_type=jnp.float32
        )
        / replicas,
        "dp",
        scatter_dimension=0,
        tiled=True,
    )
    return (query_gradient, key_gradient, value_gradient, weight_gradient)


def solution(mesh):
    in_specs = (
        P("dp", "tensor"),
        P("dp", "tensor"),
        P("dp", "tensor"),
        P(("dp", "tensor"), None),
        P("tensor", None),
        P(),
        P(),
    )
    out_specs = (P("dp", "tensor"), P("dp", "tensor"), P("dp", "tensor"), P("dp", "tensor"))
    return jax.shard_map(shards, mesh=mesh, in_specs=in_specs, out_specs=out_specs, check_vma=False)
```

profile of v0, /device:TPU:6, one launch (start us, length us, event | category | flops | bytes accessed | tf_op | source)
XLA Modules:
  0.0 1565.9 jit_solution(10318376641476542434)
XLA Ops:
  8.2 25.7 %all-gather.2.cloned.1.call-done = bf16[1024,5120]{1,0:T(8,128)(2,1)} async-done(((bf16[512,5120]{1,0:T(8,128)(2,1)}), bf16[1024,5120]{1,0:T(8,128)(2,1)}) %all-gather.2.cloned.1.call-update) | async-done | bytes 10485776 | tf_op jit(solution)/shard_map/all_gather | solution.py:153
  33.9 23.3 %convolution_convert_fusion = bf16[1024,1536]{1,0:T(8,128)(2,1)} fusion(bf16[1024,5120]{1,0:T(8,128)(2,1)} %all-gather.2.cloned.1.call-done, bf16[1536,5120]{1,0:T(8,128)(2,1)} %param.37), kind=kOutput, calls=%fused_computation.57 | convolution fusion | flops 16107700224 | bytes 29360128 | tf_op jit(solution)/shard_map/dot_general | solution.py:154
  57.3 3.5 broadcast.83.clone2
  60.7 3.4 broadcast.83.clone
  64.1 795.3 %while.16 = (s32[]{:T(128)}, f32[1024,1536]{1,0:T(8,128)}, f32[1024,1536]{1,0:T(8,128)}, bf16[8,128,1536]{1,2,0:T(8,128)(2,1)}, bf16[8,128,1536]{2,1,0:T(8,128)(...) while((s32[]{:T(128)}, f32[1024,1536]{1,0:T(8,128)}, ...), condition=%wide.region_32.33_spmd, body=%wide.region_0.32_spmd.sunk | while | flops 1235676672 | bytes 212910320 | solution.py:144
  112.6 3.0 multiply_reduce_fusion.2
  115.6 4.3 fusion.83
  123.4 2.9 conditional.33
  132.1 4.8 conditional.35
  140.5 5.9 constant_dynamic-slice_fusion.15
  148.8 4.0 maximum_add_fusion.4
  159.4 4.2 maximum_add_fusion.5
  216.4 3.0 multiply_reduce_fusion.2
  219.4 4.3 fusion.83
  227.2 2.9 conditional.33
  235.9 4.8 conditional.35
  244.3 5.9 constant_dynamic-slice_fusion.15
  252.6 4.0 maximum_add_fusion.4
  263.2 4.2 maximum_add_fusion.5
  320.2 3.0 multiply_reduce_fusion.2
  323.2 4.3 fusion.83
  331.0 2.9 conditional.33
  339.7 4.8 conditional.35
  348.1 5.9 constant_dynamic-slice_fusion.15
  356.4 4.0 maximum_add_fusion.4
  367.0 4.2 maximum_add_fusion.5
  421.1 3.0 multiply_reduce_fusion.2
  424.1 4.3 fusion.83
  437.8 4.8 conditional.35
  446.3 5.9 constant_dynamic-slice_fusion.15
  454.6 4.0 maximum_add_fusion.4
  465.2 4.2 maximum_add_fusion.5
  519.1 3.0 multiply_reduce_fusion.2
  522.1 4.3 fusion.83
  531.5 2.9 conditional.34
  535.9 4.8 conditional.35
  544.3 5.9 constant_dynamic-slice_fusion.15
  552.6 4.0 maximum_add_fusion.4
  563.2 4.2 maximum_add_fusion.5
  616.3 3.0 multiply_reduce_fusion.2
  619.3 4.3 fusion.83
  641.3 5.9 constant_dynamic-slice_fusion.15
  649.6 4.0 maximum_add_fusion.4
  660.3 4.2 maximum_add_fusion.5
  713.4 3.0 multiply_reduce_fusion.2
  716.3 4.3 fusion.83
  738.4 5.9 constant_dynamic-slice_fusion.15
  746.7 4.0 maximum_add_fusion.4
  757.3 4.2 maximum_add_fusion.5
  792.6 4.4 conditional.24
  809.5 3.0 multiply_reduce_fusion.2
  812.5 4.3 fusion.83
  818.7 3.1 conditional.32
  832.0 5.9 constant_dynamic-slice_fusion.15
  840.3 4.0 maximum_add_fusion.4
  851.0 4.2 maximum_add_fusion.5
  859.4 25.3 %multiply_bitcast_fusion = f32[5120,1536]{0,1:T(8,128)} fusion(bf16[1024,1536]{1,0:T(8,128)(2,1)} %bitcast.47, bf16[1024,5120]{1,0:T(8,128)(2,1)} %all-gather.2.cloned.1.call-done), kind=kOutput, calls=%fused_computation.55 | convolution fusion | flops 16113991680 | bytes 45088768 | tf_op jit(solution)/shard_map/dot_general | solution.py:183
  884.7 30.7 %copy.104 = f32[5120,1536]{1,0:T(8,128)} copy(f32[5120,1536]{0,1:T(8,128)} %multiply_bitcast_fusion) | data formatting | bytes 62914560
  915.5 3.3 convert_element_type.49
  935.0 148.4 %collective-permute-done.2 = bf16[512,1536]{1,0:T(8,128)(2,1)} collective-permute-done((bf16[512,1536]{1,0:T(8,128)(2,1)}, bf16[512,1536]{1,0:T(8,128)(2,1)}, u32[]{:S(2)}, u32[]{:S(2)}) %collective-permute-start.2) | collective-permute-done | bytes 1572896 | tf_op jit(solution)/shard_map/ppermute | solution.py:14
  1088.0 99.4 %collective-permute-done.1 = bf16[512,1536]{1,0:T(8,128)(2,1)} collective-permute-done((bf16[512,1536]{1,0:T(8,128)(2,1)}, bf16[512,1536]{1,0:T(8,128)(2,1)}, u32[]{:S(2)}, u32[]{:S(2)}) %collective-permute-start.1) | collective-permute-done | bytes 1572896 | tf_op jit(solution)/shard_map/ppermute | solution.py:14
  1187.4 100.3 %collective-permute-done = bf16[512,1536]{1,0:T(8,128)(2,1)} collective-permute-done((bf16[512,1536]{1,0:T(8,128)(2,1)}, bf16[512,1536]{1,0:T(8,128)(2,1)}, u32[]{:S(2)}, u32[]{:S(2)}) %collective-permute-start) | collective-permute-done | bytes 1572896 | tf_op jit(solution)/shard_map/ppermute | solution.py:14
  1290.3 2.9 pad_maximum_fusion
  1293.3 265.8 %reduce-scatter.4.cloned.1.call-done = f32[320,1536]{1,0:T(8,128)} async-done(((f32[5120,1536]{1,0:T(8,128)}), f32[320,1536]{1,0:T(8,128)}) %reduce-scatter.4.cloned.1.call-update) | async-done | bytes 1966096
  (1034 shorter events, 719.7 us)
Async XLA Ops:
  7.2 26.7 %all-gather.2.cloned.1.call-start = ((), (), s32[]{:S(2)}) async-start(), calls=%async_computation.1 | async-start | bytes 15728640 | tf_op jit(solution)/shard_map/all_gather | solution.py:153
  7.9 1551.1 %reduce-scatter.4.cloned.1.call-start = ((), (), s32[]{:S(2)}) async-start(), calls=%async_computation.2 | async-start | bytes 33423360
  64.1 5.8 copy-start.33
  83.4 9.3 copy-start.7
  84.5 5.7 copy-start.5
  84.8 5.4 copy-start.9
  95.2 3.6 copy-start.30
  95.2 3.6 copy-start.31
  131.6 5.4 copy-start.13
  131.6 5.4 copy-start.17
  136.9 9.5 copy-start.21
  167.9 5.8 copy-start.33
  187.2 9.3 copy-start.7
  188.3 5.7 copy-start.5
  188.6 5.4 copy-start.9
  199.0 3.6 copy-start.30
  199.0 3.6 copy-start.31
  235.4 5.4 copy-start.13
  235.4 5.4 copy-start.17
  240.7 9.5 copy-start.21
  271.7 5.8 copy-start.33
  291.0 9.3 copy-start.7
  292.1 5.7 copy-start.5
  292.4 5.4 copy-start.9
  302.8 3.6 copy-start.30
  339.2 5.4 copy-start.13
  339.2 5.4 copy-start.17
  344.5 9.5 copy-start.21
  375.5 5.8 copy-start.33
  394.8 9.3 copy-start.7
  395.9 5.7 copy-start.5
  396.2 5.4 copy-start.9
  437.3 5.4 copy-start.13
  437.3 5.4 copy-start.17
  442.7 9.5 copy-start.21
  473.6 5.8 copy-start.33
  492.8 9.3 copy-start.7
  494.0 5.7 copy-start.5
  494.2 5.4 copy-start.9
  535.3 5.4 copy-start.13
  535.3 5.4 copy-start.17
  540.7 9.5 copy-start.21
  571.6 5.8 copy-start.33
  590.9 6.8 copy-start.7
  600.2 3.6 copy-start.30
  600.2 3.6 copy-start.31
  637.7 9.5 copy-start.21
  668.7 5.8 copy-start.33
  687.9 6.8 copy-start.7
  734.8 9.5 copy-start.21
  765.8 5.8 copy-start.33
  785.0 6.3 copy-start.7
  792.3 6.1 copy-start.30
  792.3 6.1 copy-start.31
  828.5 9.5 copy-start.21
  915.5 4.6 slice-start
  915.5 5.4 slice-start.1
  920.1 163.3 %collective-permute-start.2 = (bf16[512,1536]{1,0:T(8,128)(2,1)}, bf16[512,1536]{1,0:T(8,128)(2,1)}, u32[]{:S(2)}, u32[]{:S(2)}) collective-permute-start(bf16[512,1536]{1,0:T(8,128)(2,1)} %slice.156), channel_id=1, source_target_pairs={{0,16},{2,18},{4,20},{6,22},{8,24},{10,26},{12,28},{14,30},{16,0},... | collective-permute-start | bytes 4718600 | tf_op jit(solution)/shard_map/ppermute | solution.py:14
  923.1 264.4 %collective-permute-start.1 = (bf16[512,1536]{1,0:T(8,128)(2,1)}, bf16[512,1536]{1,0:T(8,128)(2,1)}, u32[]{:S(2)}, u32[]{:S(2)}) collective-permute-start(bf16[512,1536]{1,0:T(8,128)(2,1)} %slice.154), channel_id=1, source_target_pairs={{0,16},{2,18},{4,20},{6,22},{8,24},{10,26},{12,28},{14,30},{16,0},... | collective-permute-start | bytes 4718600 | tf_op jit(solution)/shard_map/ppermute | solution.py:14
  927.1 3.8 copy-start.32
  929.7 358.1 %collective-permute-start = (bf16[512,1536]{1,0:T(8,128)(2,1)}, bf16[512,1536]{1,0:T(8,128)(2,1)}, u32[]{:S(2)}, u32[]{:S(2)}) collective-permute-start(bf16[512,1536]{1,0:T(8,128)(2,1)} %bitcast.191), channel_id=1, source_target_pairs={{0,16},{2,18},{4,20},{6,22},{8,24},{10,26},{12,28},{14,30},{16,0},... | collective-permute-start | bytes 4718600 | tf_op jit(solution)/shard_map/ppermute | solution.py:14
  1086.1 201.7 %copy-start.26 = (bf16[4,128,1536]{2,1,0:T(8,128)(2,1)S(1)}, bf16[4,128,1536]{2,1,0:T(8,128)(2,1)}, u32[]{:S(2)}) copy-start(bf16[4,128,1536]{2,1,0:T(8,128)(2,1)} %copy.83) | copy-start | bytes 4718596
  1088.0 202.3 %copy-start.27 = (bf16[4,128,1536]{2,1,0:T(8,128)(2,1)S(1)}, bf16[4,128,1536]{2,1,0:T(8,128)(2,1)}, u32[]{:S(2)}) copy-start(bf16[4,128,1536]{2,1,0:T(8,128)(2,1)} %copy.82) | copy-start | bytes 4718596
  1290.3 268.7 %copy-start.1 = (s32[16,8]{0,1:T(8,128)S(1)}, s32[16,8]{0,1:T(8,128)}, u32[]{:S(2)}) copy-start(s32[16,8]{0,1:T(8,128)} %param.38) | copy-start | bytes 1540
  (167 other events, 289.0 us)
Sparse Core Ops, SparseCore 0:
  9.6 24.2 all-gather.1
  915.6 643.3 reduce-scatter.3
where the time goes:
time: 1580 us; the launch traced here: 1570 us
  waiting for transfers between devices  640 us (41%)
  local copies, waits for them, and re-layouts  419 us (27%)
  other arithmetic  222 us (14%)
  matrix products  195 us (12%)
  loops' own time  70.8 us (4%)
    ppermute x3, waiting for transfers between devices, swapped(): lax.ppermute(x, axis, [(i, i ^ 1 << distance) for i in range(lax.axis_siz...  348 us
    unnamed x3, waiting for transfers between devices  266 us
    while x496, local copies, waits for them, and re-layouts  88.6 us
    another operation x1, loops' own time, attend(): lax.scan(visit, start_totals, jnp.arange(total_blocks, dtype=jnp.int32))  70.1 us
    dynamic_slice x16, local copies, waits for them, and re-layouts, visit(): lax.dynamic_slice_in_dim(value_total, start * BLOCK, window * BLOCK, 0)  66.3 us
    dot_general x18, matrix products, visit(): jnp.einsum('hqk,khd->qhd', weight_tile, value_tile, preferred_element_typ...  42.8 us
    another operation x58, local copies, waits for them, and re-layouts  42 us
    convert_element_type x8, other arithmetic, visit(): score_gradient = (chances * (chance_gradient - jnp.transpose(centering)[:...  34.5 us
  transfers between devices with their start and end apart: 5, of which 5 were waited for; matrix products, arithmetic and copies ran while one was open for 2% of the time, Pallas kernels for 0%

commit v1 on v0

v1 whole, which is shorter than its diff:
```python
import functools
import math

import jax
import jax.numpy as jnp
from jax import lax
from jax.experimental import pallas as pl
from jax.experimental.pallas import tpu as pltpu
from jax.sharding import PartitionSpec as P

HEAD_SIZE = 128
BLOCK = 128

masked_score = -1e30


def contract(a, b, dims):
    return lax.dot_general(a, b, (dims, ((), ())), preferred_element_type=jnp.float32)


def attend_kernel(
    window, starts, same, q_ref, k_ref, v_ref, g_ref, lead_ref, trail_ref, out_ref, key_sum, value_sum
):
    length = q_ref.shape[0]
    blocks = length // BLOCK
    half = lead_ref.shape[1]
    scale = HEAD_SIZE ** (-0.5)
    exponent = scale * math.log2(math.e)
    key_sum[...] = jnp.zeros_like(key_sum)
    value_sum[...] = jnp.zeros_like(value_sum)
    for index in range(blocks):
        rows = slice(index * BLOCK, (index + 1) * BLOCK)
        span = pl.ds(pl.multiple_of(starts[index] * BLOCK, BLOCK), window * BLOCK)
        query, grad = q_ref[rows, :], g_ref[rows, :]
        keys, values = k_ref[span, :], v_ref[span, :]
        raw = contract(keys, query, ((1,), (1,))) * exponent
        scores = jnp.concatenate(
            [
                raw[tile * BLOCK : (tile + 1) * BLOCK]
                + jnp.where(same[index * window + tile] == 1, 0.0, masked_score)
                for tile in range(window)
            ],
            axis=0,
        )
        weights = jnp.exp2(scores - jnp.max(scores, axis=0, keepdims=True))
        chances = weights * (1.0 / jnp.sum(weights, axis=0, keepdims=True))
        chance_weights = chances.astype(jnp.bfloat16)
        output = contract(values, chance_weights, ((0,), (0,))).astype(jnp.bfloat16)
        grad_turned = grad.astype(jnp.float32).T
        centering = jnp.sum(grad_turned * output.astype(jnp.float32), axis=0, keepdims=True)
        chance_gradient = contract(values, grad, ((1,), (1,)))
        slopes = (chances * (chance_gradient - centering)).astype(jnp.bfloat16)
        query_turned = contract(keys, slopes, ((0,), (0,))) * scale
        out_ref[rows, :] = output.astype(jnp.float32).T.astype(jnp.bfloat16)
        query_local = query_turned.T.astype(jnp.bfloat16)
        if index * BLOCK < half:
            lead_ref[0, rows, :] = query_local
        else:
            trail_ref[0, index * BLOCK - half : (index + 1) * BLOCK - half, :] = query_local
        key_sum[span, :] += contract(slopes, query, ((1,), (0,)))
        value_sum[span, :] += contract(chance_weights, grad, ((1,), (0,)))
    key_local = (key_sum[...] * scale).astype(jnp.bfloat16)
    value_local = value_sum[...].astype(jnp.bfloat16)
    lead_ref[1] = key_local[:half]
    trail_ref[1] = key_local[half:]
    lead_ref[2] = value_local[:half]
    trail_ref[2] = value_local[half:]


def attend(query, key_rows, value, gradient, starts, same, first, heads, window, trailing):
    length = query.shape[0]
    columns = heads * HEAD_SIZE
    lead = length - trailing
    whole = pl.BlockSpec((length, HEAD_SIZE), lambda head, *_: (0, head + first))
    own = pl.BlockSpec((length, HEAD_SIZE), lambda head, *_: (0, head))
    return pl.pallas_call(
        functools.partial(attend_kernel, window),
        out_shape=(
            jax.ShapeDtypeStruct((3, lead, columns), jnp.bfloat16),
            jax.ShapeDtypeStruct((3, trailing, columns), jnp.bfloat16),
            jax.ShapeDtypeStruct((length, columns), jnp.bfloat16),
        ),
        grid_spec=pltpu.PrefetchScalarGridSpec(
            num_scalar_prefetch=2,
            grid=(heads,),
            in_specs=[whole, whole, whole, own],
            out_specs=(
                pl.BlockSpec((3, lead, HEAD_SIZE), lambda head, *_: (0, 0, head)),
                pl.BlockSpec((3, trailing, HEAD_SIZE), lambda head, *_: (0, 0, head)),
                own,
            ),
            scratch_shapes=[
                pltpu.VMEM((length, HEAD_SIZE), jnp.float32),
                pltpu.VMEM((length, HEAD_SIZE), jnp.float32),
            ],
        ),
        compiler_params=pltpu.CompilerParams(vmem_limit_bytes=32 * 1024 * 1024),
        cost_estimate=pl.CostEstimate(
            flops=10 * length * window * BLOCK * columns,
            bytes_accessed=16 * length * columns,
            transcendentals=length * window * BLOCK * heads,
        ),
    )(starts, same, query, key_rows, value, gradient)


def shards(queries, keys, values, out_gradient, out_weight, segments, counts):
    full_gradient = lax.all_gather(out_gradient, "tensor", axis=0, tiled=True)
    replicas = lax.axis_size("dp")
    halfway = replicas // 2
    position = lax.axis_index("dp")
    blocks = segments.shape[1]
    window = blocks // 2
    trailing = window * BLOCK
    heads = queries.shape[1] // HEAD_SIZE
    groups = max(count for count in (1, 2, 3) if heads % count == 0)
    each = heads // groups
    moving = lax.dynamic_index_in_dim(counts, position, 0, keepdims=False)
    ids = lax.dynamic_index_in_dim(segments, position, 0, keepdims=False)
    firsts = jnp.argmax(ids[:, None] == ids[None, :], axis=1).astype(jnp.int32)
    starts = jnp.minimum(firsts, blocks - window)
    near = jnp.take(ids, starts[:, None] + jnp.arange(window, dtype=jnp.int32)[None, :])
    same = (near == ids[:, None]).astype(jnp.int32).reshape(-1)
    block_moved = jnp.arange(blocks, dtype=jnp.int32) >= blocks - moving
    row_moved = jnp.repeat(block_moved, BLOCK)[-trailing:, None]
    pairs = [(i, (i + halfway) % replicas) for i in range(replicas)]

    leads, trails, weight_parts = [], [], []
    for group in range(groups):
        width = each * HEAD_SIZE
        head_gradient = contract(
            full_gradient, out_weight[group * width : (group + 1) * width], ((1,), (1,))
        ).astype(jnp.bfloat16)
        lead, trail, head_output = attend(
            queries, keys, values, head_gradient, starts, same, group * each, each, window, trailing
        )
        arrived = lax.ppermute(trail, "dp", pairs)
        leads.append(lead)
        trails.append((trail, arrived))
        term = (contract(full_gradient, head_output, ((0,), (0,))) / replicas).astype(jnp.bfloat16)
        weight_parts.append(lax.psum_scatter(term, "dp", scatter_dimension=0, tiled=True))

    def settled(which):
        upper = jnp.concatenate([lead[which] for lead in leads], axis=1)
        lower = jnp.concatenate(
            [jnp.where(row_moved, arrived[which], trail[which]) for trail, arrived in trails], axis=1
        )
        return jnp.concatenate([upper, lower], axis=0)

    weight_gradient = jnp.concatenate(weight_parts, axis=1).astype(jnp.float32)
    return (settled(0), settled(1), settled(2), weight_gradient)


def solution(mesh):
    in_specs = (
        P("dp", "tensor"),
        P("dp", "tensor"),
        P("dp", "tensor"),
        P(("dp", "tensor"), None),
        P("tensor", None),
        P(),
        P(),
    )
    out_specs = (P("dp", "tensor"), P("dp", "tensor"), P("dp", "tensor"), P("dp", "tensor"))
    return jax.shard_map(shards, mesh=mesh, in_specs=in_specs, out_specs=out_specs, check_vma=False)
```

time: 1580 us -> 556 us (0.35)
  local copies, waits for them, and re-layouts: 419 us -> 38.7 us
  waiting for transfers between devices: 640 us -> 317 us
  other arithmetic: 222 us -> 42.7 us
  matrix products: 195 us -> 60.7 us
  loops' own time: 70.8 us -> 0 us
  Pallas kernels: 0 us -> 67.4 us
    unnamed x3 -> x7, waiting for transfers between devices: 266 us -> 0.77 us
    dot_general x110 -> x6, matrix products: 195 us -> 60.7 us  [contract(): lax.dot_general(a, b, (dims, ((), ())), preferred_element_type=jnp.float32)]
    dynamic_slice x73 -> x1, local copies, waits for them, and re-layouts: 108 us -> 0.18 us  [shards(): ids = lax.dynamic_index_in_dim(segments, position, 0, keepdims=False)]
    dynamic_update_slice x56 -> x0, local copies, waits for them, and re-layouts: 95.6 us -> none  [the longest x16 34.1 us: visit(): lax.dynamic_update_slice_in_dim(value_total, lax.dynamic_slice_in_dim(val...]
    while x496 -> x0, local copies, waits for them, and re-layouts: 88.6 us -> none
    another operation x97 -> x0, loops' own time: 70.8 us -> none  [the longest x1 70.1 us: attend(): lax.scan(visit, start_totals, jnp.arange(total_blocks, dtype=jnp.int32))]
    convert_element_type x26 -> x2, other arithmetic: 69.4 us -> 0.17 us  [the longest x1 0.16 us: shards(): weight_gradient = jnp.concatenate(weight_parts, axis=1).astype(jnp.float32)]
    pallas_call x0 -> x3, Pallas kernels: none -> 67.4 us  [attend(): pl.pallas_call(functools.partial(attend_kernel, window), out_shape=(jax.S...]
  transfers between devices with their start and end apart: 5 -> 7, of which waited for: 5 -> 4; matrix products, arithmetic and copies ran while one was open for 2% -> 19% of each run, Pallas kernels for 0% -> 8%
where the time goes in v1:
time: 556 us; the launch traced here: 548 us
  waiting for transfers between devices  317 us (57%)
  Pallas kernels  67.4 us (12%)
  matrix products  60.7 us (11%)
  other arithmetic  42.7 us (8%)
  local copies, waits for them, and re-layouts  38.7 us (7%)
  between operations  15.3 us (3%)
  starting transfers between devices  6.23 us (1%)
    ppermute x3, waiting for transfers between devices, shards(): arrived = lax.ppermute(trail, 'dp', pairs)  292 us
    pallas_call x3, Pallas kernels, attend(): pl.pallas_call(functools.partial(attend_kernel, window), out_shape=(jax.S...  67.4 us
    dot_general x6, matrix products, contract(): lax.dot_general(a, b, (dims, ((), ())), preferred_element_type=jnp.float32)  60.7 us
    concatenate x2, other arithmetic, settled(): return jnp.concatenate([upper, lower], axis=0)  40.9 us
    unnamed x53, local copies, waits for them, and re-layouts  36.2 us
    all_gather x1, waiting for transfers between devices, shards(): full_gradient = lax.all_gather(out_gradient, 'tensor', axis=0, tiled=True)  23.8 us
  transfers between devices with their start and end apart: 7, of which 4 were waited for; matrix products, arithmetic and copies ran while one was open for 19% of the time, Pallas kernels for 8%

profile of v1, /device:TPU:6, one launch (start us, length us, event | category | flops | bytes accessed | tf_op | source)
XLA Modules:
  0.0 547.8 jit_solution(4189924622464781837)
XLA Ops:
  7.2 0.0 copy-start
  7.2 0.0 all-gather.2.cloned.1.call-start
  7.2 0.7 all-gather.2.cloned.1.call-update
  7.9 0.0 reduce-scatter.12.cloned.1.call-start
  8.0 0.2 dynamic-slice_reduce_fusion
  8.2 0.7 iota_reduce_fusion
  8.9 0.1 compare_select_fusion
  8.9 0.1 reshape.75
  9.0 0.7 gather_fusion
  9.7 0.1 add.68
  9.8 0.1 add.69
  9.9 0.1 eq.32
  10.0 0.1 eq.33
  10.0 0.1 add.71
  10.2 23.8 %all-gather.2.cloned.1.call-done = bf16[1024,5120]{1,0:T(8,128)(2,1)} async-done(((bf16[512,5120]{1,0:T(8,128)(2,1)}), bf16[1024,5120]{1,0:T(8,128)(2,1)}) %all-gather.2.cloned.1.call-update) | async-done | bytes 10485776 | tf_op jit(solution)/shard_map/all_gather | solution.py:107
  33.9 10.0 %fusion.12.g_ref = bf16[1024,512]{1,0:T(8,128)(2,1)S(1)} fusion(bf16[1024,5120]{1,0:T(8,128)(2,1)} %all-gather.2.cloned.1.call-done, bf16[1536,5120]{1,0:T(8,128)(2,1)} %param.11), kind=kOutput, calls=%fused_computation.17 | convolution fusion | flops 5369233408 | bytes 16777216 | tf_op jit(solution)/shard_map/dot_general | solution.py:18
  44.0 22.5 %shard_map.103 = (bf16[3,512,512]{2,1,0:T(8,128)(2,1)S(1)}, bf16[3,512,512]{2,1,0:T(8,128)(2,1)S(1)}, bf16[1024,512]{1,0:T(8,128)(2,1)S(1)}) custom-call(s32[8]{0:T(128)S(1)} %broadcast_minimum_fusion.starts, s32[32]{0:T(128)S(1)} %compare_convert_fusion.same, bf16[1024,1536]{1,0:T(8,128)(2,1)S(1)} %copy-done.2, bf16[1024,1536]{1,0:T(8,128)(2,1)S(1)} %copy-done.3, ...), custom_call_target="tpu_custom_call" | custom-call | flops 2684354560 | bytes 8388608 | tf_op jit(solution)/shard_map/pallas_call | solution.py:76
  66.5 1.1 copy-done.9
  67.6 1.1 copy-done.15
  68.7 7.6 %fusion.1 = bf16[5120,512]{0,1:T(8,128)(2,1)} fusion(bf16[1024,512]{1,0:T(8,128)(2,1)S(1)} %get-tuple-element.22, bf16[1024,5120]{1,0:T(8,128)(2,1)S(1)} %copy-done.21), kind=kOutput, calls=%fused_computation.5 | convolution fusion | flops 5373952000 | bytes 16777216 | tf_op jit(solution)/shard_map/dot_general | solution.py:18
  76.4 8.0 %copy.17 = bf16[5120,512]{1,0:T(8,128)(2,1)} copy(bf16[5120,512]{0,1:T(8,128)(2,1)} %fusion.1) | data formatting | bytes 10485760
  84.3 0.0 reduce-scatter.12.cloned.1.call-update
  84.4 0.5 reduce-scatter.14.cloned.1.call-start
  84.9 0.0 copy-start.4
  84.9 0.0 copy-start.7
  84.9 10.0 %fusion.15.g_ref = bf16[1024,512]{1,0:T(8,128)(2,1)S(1)} fusion(bf16[1024,5120]{1,0:T(8,128)(2,1)} %all-gather.2.cloned.1.call-done, bf16[1536,5120]{1,0:T(8,128)(2,1)} %param.11), kind=kOutput, calls=%fused_computation.18 | convolution fusion | flops 5369233408 | bytes 16777216 | tf_op jit(solution)/shard_map/dot_general | solution.py:18
  95.0 22.5 %shard_map.104 = (bf16[3,512,512]{2,1,0:T(8,128)(2,1)S(1)}, bf16[3,512,512]{2,1,0:T(8,128)(2,1)S(1)}, bf16[1024,512]{1,0:T(8,128)(2,1)S(1)}) custom-call(s32[8]{0:T(128)S(1)} %broadcast_minimum_fusion.starts, s32[32]{0:T(128)S(1)} %compare_convert_fusion.same, bf16[1024,1536]{1,0:T(8,128)(2,1)S(1)} %copy-done.2, bf16[1024,1536]{1,0:T(8,128)(2,1)S(1)} %copy-done.4, ...), custom_call_target="tpu_custom_call" | custom-call | flops 2684354560 | bytes 8388608 | tf_op jit(solution)/shard_map/pallas_call | solution.py:76
  117.4 0.0 copy-start.11
  117.4 1.1 copy-done.11
  118.6 1.1 copy-done.17
  119.7 11.5 %fusion.2 = bf16[5120,512]{0,1:T(8,128)(2,1)} fusion(bf16[1024,512]{1,0:T(8,128)(2,1)S(1)} %get-tuple-element.23, bf16[1024,5120]{1,0:T(8,128)(2,1)} %all-gather.2.cloned.1.call-done), kind=kOutput, calls=%fused_computation.6 | convolution fusion | flops 5373952000 | bytes 16777216 | tf_op jit(solution)/shard_map/dot_general | solution.py:18
  131.2 7.9 %copy.19 = bf16[5120,512]{1,0:T(8,128)(2,1)} copy(bf16[5120,512]{0,1:T(8,128)(2,1)} %fusion.2) | data formatting | bytes 10485760
  139.2 0.0 reduce-scatter.14.cloned.1.call-update
  139.2 0.2 reduce-scatter.10.cloned.1.call-start
  139.4 0.0 copy-start.5
  139.4 10.1 %fusion.9.g_ref = bf16[1024,512]{1,0:T(8,128)(2,1)S(1)} fusion(bf16[1024,5120]{1,0:T(8,128)(2,1)} %all-gather.2.cloned.1.call-done, bf16[1536,5120]{1,0:T(8,128)(2,1)} %param.11), kind=kOutput, calls=%fused_computation.16 | convolution fusion | flops 5369233408 | bytes 16777216 | tf_op jit(solution)/shard_map/dot_general | solution.py:18
  149.5 22.4 %shard_map.102 = (bf16[3,512,512]{2,1,0:T(8,128)(2,1)S(1)}, bf16[3,512,512]{2,1,0:T(8,128)(2,1)S(1)}, bf16[1024,512]{1,0:T(8,128)(2,1)S(1)}) custom-call(s32[8]{0:T(128)S(1)} %broadcast_minimum_fusion.starts, s32[32]{0:T(128)S(1)} %compare_convert_fusion.same, bf16[1024,1536]{1,0:T(8,128)(2,1)S(1)} %copy-done.2, bf16[1024,1536]{1,0:T(8,128)(2,1)S(1)} %copy-done.5, ...), custom_call_target="tpu_custom_call" | custom-call | flops 2684354560 | bytes 8388608 | tf_op jit(solution)/shard_map/pallas_call | solution.py:76
  172.0 1.2 copy-done.13
  173.2 1.1 copy-done.19
  174.3 11.5 %fusion = bf16[5120,512]{0,1:T(8,128)(2,1)} fusion(bf16[1024,512]{1,0:T(8,128)(2,1)S(1)} %get-tuple-element.21, bf16[1024,5120]{1,0:T(8,128)(2,1)} %all-gather.2.cloned.1.call-done), kind=kOutput, calls=%fused_computation.4 | convolution fusion | flops 5373952000 | bytes 16777216 | tf_op jit(solution)/shard_map/dot_general | solution.py:18
  185.8 7.9 %copy.15 = bf16[5120,512]{1,0:T(8,128)(2,1)} copy(bf16[5120,512]{0,1:T(8,128)(2,1)} %fusion) | data formatting | bytes 10485760
  193.7 0.0 reduce-scatter.10.cloned.1.call-update
  193.8 2.5 collective-permute-start.1
  196.3 0.5 collective-permute-start.2
  196.8 2.4 collective-permute-start
  199.2 0.7 dynamic_slice.9
  200.6 0.1 slice.101
  200.7 0.1 broadcast_bitcast_fusion
  200.7 0.1 slice_bitcast_fusion.10
  200.9 0.1 slice_bitcast_fusion.9
  201.0 0.1 slice_bitcast_fusion.11
  201.1 184.9 %collective-permute-done.1 = bf16[3,512,512]{2,1,0:T(8,128)(2,1)S(1)} collective-permute-done((bf16[3,512,512]{2,1,0:T(8,128)(2,1)}, bf16[3,512,512]{2,1,0:T(8,128)(2,1)S(1)}, u32[]{:S(2)}, u32[]{:S(2)}) %collective-permute-start.1) | collective-permute-done | bytes 1572896 | tf_op jit(solution)/shard_map/ppermute | solution.py:136
  386.0 40.7 %collective-permute-done.2 = bf16[3,512,512]{2,1,0:T(8,128)(2,1)S(1)} collective-permute-done((bf16[3,512,512]{2,1,0:T(8,128)(2,1)}, bf16[3,512,512]{2,1,0:T(8,128)(2,1)S(1)}, u32[]{:S(2)}, u32[]{:S(2)}) %collective-permute-start.2) | collective-permute-done | bytes 1572896 | tf_op jit(solution)/shard_map/ppermute | solution.py:136
  426.7 66.7 %collective-permute-done = bf16[3,512,512]{2,1,0:T(8,128)(2,1)S(1)} collective-permute-done((bf16[3,512,512]{2,1,0:T(8,128)(2,1)}, bf16[3,512,512]{2,1,0:T(8,128)(2,1)S(1)}, u32[]{:S(2)}, u32[]{:S(2)}) %collective-permute-start) | collective-permute-done | bytes 1572896 | tf_op jit(solution)/shard_map/ppermute | solution.py:136
  493.4 0.9 fusion.20
  494.4 19.9 %maximum_maximum_fusion.2 = bf16[1024,1536]{1,0:T(8,128)(2,1)} fusion(bf16[512,512]{1,0:T(8,128)(2,1)S(1)} %get-tuple-element.63, bf16[512,512]{1,0:T(8,128)(2,1)S(1)} %get-tuple-element.60, bf16[512,512]{1,0:T(8,128)(2,1)S(1)} %get-tuple-element.40, bf16[512,512]{1,0:T(8,128)(2,1)S(1)} %get-tuple-element.55, bf16[512,512]{1,0:T(8,128)(2,1)S(1)} %get-tuple-element.52, ...), kind=kLoop, calls=%fused_computation.15 | loop fusion | flops 18874368 | bytes 6291456 | tf_op jit(solution)/shard_map/concatenate | solution.py:147
  514.2 21.0 %maximum_maximum_fusion = (bf16[1024,1536]{1,0:T(8,128)(2,1)}, bf16[1024,1536]{1,0:T(8,128)(2,1)}) fusion(bf16[512,512]{1,0:T(8,128)(2,1)S(1)} %get-tuple-element.61, bf16[512,512]{1,0:T(8,128)(2,1)S(1)} %get-tuple-element.58, bf16[512,512]{1,0:T(8,128)(2,1)S(1)} %get-tuple-element.42, bf16[512,512]{1,0:T(8,128)(2,1)S(1)} %get-tuple-element.57, ...), kind=kLoop, calls=%fused_computation.13 | loop fusion | flops 37748736 | bytes 12582912 | tf_op jit(solution)/shard_map/concatenate | solution.py:147
  535.2 1.2 copy.18
  536.4 0.0 reduce-scatter.14.cloned.1.call-done
  536.5 1.2 copy.20
  537.6 0.0 reduce-scatter.10.cloned.1.call-done
  537.7 1.2 copy.16
  538.9 0.2 maximum_convert_fusion
  539.0 1.8 copy.14
  (41 shorter events, 0.1 us)
Async XLA Ops:
  7.2 0.8 copy-start
  7.2 26.7 %all-gather.2.cloned.1.call-start = ((), (), s32[]{:S(2)}) async-start(), calls=%async_computation.3 | async-start | bytes 15728640 | tf_op jit(solution)/shard_map/all_gather | solution.py:107
  7.9 527.3 %reduce-scatter.12.cloned.1.call-start = ((), (), s32[]{:S(2)}) async-start(), calls=%async_computation.5 | async-start | bytes 5570560
  10.1 33.8 %copy-start.2 = (bf16[1024,1536]{1,0:T(8,128)(2,1)S(1)}, bf16[1024,1536]{1,0:T(8,128)(2,1)}, u32[]{:S(2)}) copy-start(bf16[1024,1536]{1,0:T(8,128)(2,1)} %q_ref.5) | copy-start | bytes 9437188
  33.9 10.0 %copy-start.3 = (bf16[1024,1536]{1,0:T(8,128)(2,1)S(1)}, bf16[1024,1536]{1,0:T(8,128)(2,1)}, u32[]{:S(2)}) copy-start(bf16[1024,1536]{1,0:T(8,128)(2,1)} %k_ref.5) | copy-start | bytes 9437188
  33.9 10.1 %copy-start.6 = (bf16[1024,1536]{1,0:T(8,128)(2,1)S(1)}, bf16[1024,1536]{1,0:T(8,128)(2,1)}, u32[]{:S(2)}) copy-start(bf16[1024,1536]{1,0:T(8,128)(2,1)} %v_ref.5) | copy-start | bytes 9437188
  44.0 24.8 %copy-start.21 = (bf16[1024,5120]{1,0:T(8,128)(2,1)S(1)}, bf16[1024,5120]{1,0:T(8,128)(2,1)}, u32[]{:S(2)}) copy-start(bf16[1024,5120]{1,0:T(8,128)(2,1)} %all-gather.2.cloned.1.call-done) | copy-start | bytes 31457284
  66.5 1.1 copy-start.9
  67.6 1.1 copy-start.15
  84.4 452.1 %reduce-scatter.14.cloned.1.call-start = ((), (), s32[]{:S(2)}) async-start(), calls=%async_computation.6 | async-start | bytes 5570560
  84.9 10.1 %copy-start.4 = (bf16[1024,1536]{1,0:T(8,128)(2,1)S(1)}, bf16[1024,1536]{1,0:T(8,128)(2,1)}, u32[]{:S(2)}) copy-start(bf16[1024,1536]{1,0:T(8,128)(2,1)} %k_ref.5) | copy-start | bytes 9437188
  84.9 10.1 %copy-start.7 = (bf16[1024,1536]{1,0:T(8,128)(2,1)S(1)}, bf16[1024,1536]{1,0:T(8,128)(2,1)}, u32[]{:S(2)}) copy-start(bf16[1024,1536]{1,0:T(8,128)(2,1)} %v_ref.5) | copy-start | bytes 9437188
  117.4 1.1 copy-start.11
  118.6 1.1 copy-start.17
  139.2 398.5 %reduce-scatter.10.cloned.1.call-start = ((), (), s32[]{:S(2)}) async-start(), calls=%async_computation.4 | async-start | bytes 5570560
  139.4 10.1 %copy-start.5 = (bf16[1024,1536]{1,0:T(8,128)(2,1)S(1)}, bf16[1024,1536]{1,0:T(8,128)(2,1)}, u32[]{:S(2)}) copy-start(bf16[1024,1536]{1,0:T(8,128)(2,1)} %k_ref.5) | copy-start | bytes 9437188
  139.4 10.1 %copy-start.8 = (bf16[1024,1536]{1,0:T(8,128)(2,1)S(1)}, bf16[1024,1536]{1,0:T(8,128)(2,1)}, u32[]{:S(2)}) copy-start(bf16[1024,1536]{1,0:T(8,128)(2,1)} %v_ref.5) | copy-start | bytes 9437188
  172.0 1.2 copy-start.13
  173.1 1.1 copy-start.19
  193.7 5.5 %copy-start.22 = (s32[16]{0:T(128)S(1)}, s32[16]{0:T(128)}, u32[]{:S(2)}) copy-start(s32[16]{0:T(128)} %param.13) | copy-start | bytes 196
  193.7 7.0 %copy-start.10 = (bf16[3,512,512]{2,1,0:T(8,128)(2,1)S(1)}, bf16[3,512,512]{2,1,0:T(8,128)(2,1)}, u32[]{:S(2)}) copy-start(bf16[3,512,512]{2,1,0:T(8,128)(2,1)} %copy-done.9) | copy-start | bytes 4718596
  193.7 7.1 %copy-start.12 = (bf16[3,512,512]{2,1,0:T(8,128)(2,1)S(1)}, bf16[3,512,512]{2,1,0:T(8,128)(2,1)}, u32[]{:S(2)}) copy-start(bf16[3,512,512]{2,1,0:T(8,128)(2,1)} %copy-done.11) | copy-start | bytes 4718596
  193.7 7.2 %copy-start.14 = (bf16[3,512,512]{2,1,0:T(8,128)(2,1)S(1)}, bf16[3,512,512]{2,1,0:T(8,128)(2,1)}, u32[]{:S(2)}) copy-start(bf16[3,512,512]{2,1,0:T(8,128)(2,1)} %copy-done.13) | copy-start | bytes 4718596
  193.8 299.7 %copy-start.16 = (bf16[3,512,512]{2,1,0:T(8,128)(2,1)S(1)}, bf16[3,512,512]{2,1,0:T(8,128)(2,1)}, u32[]{:S(2)}) copy-start(bf16[3,512,512]{2,1,0:T(8,128)(2,1)} %copy-done.15) | copy-start | bytes 4718596
  193.8 299.7 %copy-start.18 = (bf16[3,512,512]{2,1,0:T(8,128)(2,1)S(1)}, bf16[3,512,512]{2,1,0:T(8,128)(2,1)}, u32[]{:S(2)}) copy-start(bf16[3,512,512]{2,1,0:T(8,128)(2,1)} %copy-done.17) | copy-start | bytes 4718596
  193.8 299.7 %copy-start.20 = (bf16[3,512,512]{2,1,0:T(8,128)(2,1)S(1)}, bf16[3,512,512]{2,1,0:T(8,128)(2,1)}, u32[]{:S(2)}) copy-start(bf16[3,512,512]{2,1,0:T(8,128)(2,1)} %copy-done.19) | copy-start | bytes 4718596
  193.8 192.2 %collective-permute-start.1 = (bf16[3,512,512]{2,1,0:T(8,128)(2,1)}, bf16[3,512,512]{2,1,0:T(8,128)(2,1)S(1)}, u32[]{:S(2)}, u32[]{:S(2)}) collective-permute-start(bf16[3,512,512]{2,1,0:T(8,128)(2,1)} %copy-done.15), channel_id=1, source_target_pairs={{0,16},{2,18},{4,20},{6,22},{8,24},{10,26},{12,28},{14,30},{16,0},... | collective-permute-start | bytes 4718600 | tf_op jit(solution)/shard_map/ppermute | solution.py:136
  196.3 230.4 %collective-permute-start.2 = (bf16[3,512,512]{2,1,0:T(8,128)(2,1)}, bf16[3,512,512]{2,1,0:T(8,128)(2,1)S(1)}, u32[]{:S(2)}, u32[]{:S(2)}) collective-permute-start(bf16[3,512,512]{2,1,0:T(8,128)(2,1)} %copy-done.17), channel_id=1, source_target_pairs={{0,16},{2,18},{4,20},{6,22},{8,24},{10,26},{12,28},{14,30},{16,0},... | collective-permute-start | bytes 4718600 | tf_op jit(solution)/shard_map/ppermute | solution.py:136
  196.8 296.6 %collective-permute-start = (bf16[3,512,512]{2,1,0:T(8,128)(2,1)}, bf16[3,512,512]{2,1,0:T(8,128)(2,1)S(1)}, u32[]{:S(2)}, u32[]{:S(2)}) collective-permute-start(bf16[3,512,512]{2,1,0:T(8,128)(2,1)} %copy-done.19), channel_id=1, source_target_pairs={{0,16},{2,18},{4,20},{6,22},{8,24},{10,26},{12,28},{14,30},{16,0},... | collective-permute-start | bytes 4718600 | tf_op jit(solution)/shard_map/ppermute | solution.py:136
  514.2 26.7 %copy-start.1 = (s32[16,8]{0,1:T(8,128)S(1)}, s32[16,8]{0,1:T(8,128)}, u32[]{:S(2)}) copy-start(s32[16,8]{0,1:T(8,128)} %param.12) | copy-start | bytes 1540
Sparse Core Ops, SparseCore 0:
  9.6 24.2 all-gather.1
  84.5 113.8 reduce-scatter.11
  200.7 195.1 reduce-scatter.13
  398.0 122.4 reduce-scatter.9

commit v2 on v1

--- a/solution.py
+++ b/solution.py
@@ -103,6 +103,66 @@
     )(starts, same, query, key_rows, value, gradient)
 
 
+def scattered(term, order):
+    replicas = lax.axis_size("dp")
+    position = lax.axis_index("dp")
+    rows, columns = term.shape[0] // replicas, term.shape[1]
+    remaining = list(reversed(range(replicas.bit_length() - 1)))
+    for bit in order:
+        place = remaining.index(bit)
+        remaining.pop(place)
+        below = len(remaining) - place
+        halves = term.reshape(1 << place, 2, (1 << below) * rows, columns)
+        mine = (position >> bit) & 1
+        sent = lax.dynamic_index_in_dim(halves, 1 - mine, 1, keepdims=False)
+        kept = lax.dynamic_index_in_dim(halves, mine, 1, keepdims=False)
+        arrived = lax.ppermute(sent, "dp", [(i, i ^ 1 << bit) for i in range(replicas)])
+        total = kept.astype(jnp.float32) + arrived.astype(jnp.float32)
+        term = total.reshape(-1, columns)
+        if remaining:
+            term = term.astype(jnp.bfloat16)
+    return term
+
+
+def settle_kernel(blocks, moving, lead_ref, trail_ref, arrived_ref, *refs):
+    outs = refs[-3:]
+    half = lead_ref.shape[1]
+    for which in range(3):
+        outs[which][:half, :] = lead_ref[which]
+        for block in range(trail_ref.shape[1] // BLOCK):
+            rows = slice(block * BLOCK, (block + 1) * BLOCK)
+            moved = half // BLOCK + block >= blocks - moving[0]
+
+            @pl.when(moved)
+            def _():
+                outs[which][half + block * BLOCK : half + (block + 1) * BLOCK, :] = arrived_ref[which, rows]
+
+            @pl.when(jnp.logical_not(moved))
+            def _():
+                outs[which][half + block * BLOCK : half + (block + 1) * BLOCK, :] = trail_ref[which, rows]
+
+
+def settle(moving, lead, trail, arrived, first, heads, shape, earlier):
+    step = lambda rows: pl.BlockSpec((3, rows, HEAD_SIZE), lambda head, *_: (0, 0, head))
+    length = shape[0]
+    return pl.pallas_call(
+        functools.partial(settle_kernel, length // BLOCK),
+        out_shape=(jax.ShapeDtypeStruct(shape, jnp.bfloat16),) * 3,
+        grid_spec=pltpu.PrefetchScalarGridSpec(
+            num_scalar_prefetch=1,
+            grid=(heads,),
+            in_specs=[step(lead.shape[1]), step(trail.shape[1]), step(trail.shape[1])]
+            + [pl.BlockSpec(memory_space=pl.ANY)] * len(earlier),
+            out_specs=(pl.BlockSpec((length, HEAD_SIZE), lambda head, *_: (0, head + first)),) * 3,
+        ),
+        input_output_aliases={4 + which: which for which in range(len(earlier))},
+        compiler_params=pltpu.CompilerParams(vmem_limit_bytes=32 * 1024 * 1024),
+        cost_estimate=pl.CostEstimate(
+            flops=0, bytes_accessed=15 * length * heads * HEAD_SIZE, transcendentals=0
+        ),
+    )(moving.reshape(1), lead, trail, arrived, *earlier)
+
+
 def shards(queries, keys, values, out_gradient, out_weight, segments, counts):
     full_gradient = lax.all_gather(out_gradient, "tensor", axis=0, tiled=True)
     replicas = lax.axis_size("dp")
@@ -112,7 +172,7 @@
     window = blocks // 2
     trailing = window * BLOCK
     heads = queries.shape[1] // HEAD_SIZE
-    groups = max(count for count in (1, 2, 3) if heads % count == 0)
+    groups = 2 if heads % 2 == 0 else min(heads, 3)
     each = heads // groups
     moving = lax.dynamic_index_in_dim(counts, position, 0, keepdims=False)
     ids = lax.dynamic_index_in_dim(segments, position, 0, keepdims=False)
@@ -120,11 +180,11 @@
     starts = jnp.minimum(firsts, blocks - window)
     near = jnp.take(ids, starts[:, None] + jnp.arange(window, dtype=jnp.int32)[None, :])
     same = (near == ids[:, None]).astype(jnp.int32).reshape(-1)
-    block_moved = jnp.arange(blocks, dtype=jnp.int32) >= blocks - moving
-    row_moved = jnp.repeat(block_moved, BLOCK)[-trailing:, None]
     pairs = [(i, (i + halfway) % replicas) for i in range(replicas)]
-
-    leads, trails, weight_parts = [], [], []
+    upward = list(range(replicas.bit_length() - 1))
+    orders = [upward, [1, 0] + upward[2:]]
+
+    moves, weight_parts = [], []
     for group in range(groups):
         width = each * HEAD_SIZE
         head_gradient = contract(
@@ -133,21 +193,16 @@
         lead, trail, head_output = attend(
             queries, keys, values, head_gradient, starts, same, group * each, each, window, trailing
         )
-        arrived = lax.ppermute(trail, "dp", pairs)
-        leads.append(lead)
-        trails.append((trail, arrived))
+        moves.append((lead, trail, lax.ppermute(trail, "dp", pairs)))
         term = (contract(full_gradient, head_output, ((0,), (0,))) / replicas).astype(jnp.bfloat16)
-        weight_parts.append(lax.psum_scatter(term, "dp", scatter_dimension=0, tiled=True))
-
-    def settled(which):
-        upper = jnp.concatenate([lead[which] for lead in leads], axis=1)
-        lower = jnp.concatenate(
-            [jnp.where(row_moved, arrived[which], trail[which]) for trail, arrived in trails], axis=1
+        weight_parts.append(scattered(term, orders[group % 2]))
+
+    settled = ()
+    for group, (lead, trail, arrived) in enumerate(moves):
+        settled = settle(
+            moving, lead, trail, arrived, group * each, each, queries.shape, settled
         )
-        return jnp.concatenate([upper, lower], axis=0)
-
-    weight_gradient = jnp.concatenate(weight_parts, axis=1).astype(jnp.float32)
-    return (settled(0), settled(1), settled(2), weight_gradient)
+    return (*settled, jnp.concatenate(weight_parts, axis=1))
 
 
 def solution(mesh):

time: 556 us -> 584 us (1.050)
  local copies, waits for them, and re-layouts: 38.7 us -> 102 us
  waiting for transfers between devices: 317 us -> 292 us
  other arithmetic: 42.7 us -> 19.8 us
  Pallas kernels: 67.4 us -> 80.1 us
  starting transfers between devices: 6.23 us -> 15.5 us
    concatenate x2 -> x1, other arithmetic: 40.9 us -> 1.54 us  [shards(): return (*settled, jnp.concatenate(weight_parts, axis=1))]
    ppermute x3 -> x10, waiting for transfers between devices: 292 us -> 268 us  [the longest x8 205 us: scattered(): lax.ppermute(sent, 'dp', [(i, i ^ 1 << bit) for i in range(replicas)])]
    dynamic_slice x0 -> x1, local copies, waits for them, and re-layouts: none -> 19 us  [scattered(): kept = lax.dynamic_index_in_dim(halves, mine, 1, keepdims=False)]
    reshape x0 -> x1, local copies, waits for them, and re-layouts: none -> 17.9 us  [scattered(): halves = term.reshape(1 << place, 2, (1 << below) * rows, columns)]
    convert_element_type x1 -> x6, other arithmetic: 0.16 us -> 15.2 us  [scattered(): term = term.astype(jnp.bfloat16)]
    pallas_call x0 -> x2, Pallas kernels: none -> 13.3 us  [settle(): pl.pallas_call(functools.partial(settle_kernel, length // BLOCK), out_sha...]
    convert_element_type x0 -> x1, local copies, waits for them, and re-layouts: none -> 10.7 us  [shards(): (contract(full_gradient, head_output, ((0,), (0,))) / replicas).astype(jn...]
    ppermute x3 -> x10, starting transfers between devices: 5.43 us -> 15.4 us  [the longest x8 12.5 us: scattered(): lax.ppermute(sent, 'dp', [(i, i ^ 1 << bit) for i in range(replicas)])]
  transfers between devices with their start and end apart: 7 -> 11, of which waited for: 4 -> 10; matrix products, arithmetic and copies ran while one was open for 19% -> 21% of each run, Pallas kernels for 8% -> 8%
where the time goes in v2:
time: 584 us; the launch traced here: 581 us
  waiting for transfers between devices  292 us (50%)
  local copies, waits for them, and re-layouts  102 us (17%)
  Pallas kernels  80.1 us (14%)
  matrix products  56.7 us (10%)
  other arithmetic  19.8 us (3%)
  starting transfers between devices  15.5 us (3%)
  between operations  14.3 us (2%)
    ppermute x8, waiting for transfers between devices, scattered(): lax.ppermute(sent, 'dp', [(i, i ^ 1 << bit) for i in range(replicas)])  205 us
    pallas_call x2, Pallas kernels, attend(): pl.pallas_call(functools.partial(attend_kernel, window), out_shape=(jax.S...  66.8 us
    ppermute x2, waiting for transfers between devices, shards(): moves.append((lead, trail, lax.ppermute(trail, 'dp', pairs)))  62.5 us
    dot_general x4, matrix products, contract(): lax.dot_general(a, b, (dims, ((), ())), preferred_element_type=jnp.float32)  56.7 us
    unnamed x50, local copies, waits for them, and re-layouts  42.6 us
    all_gather x1, waiting for transfers between devices, shards(): full_gradient = lax.all_gather(out_gradient, 'tensor', axis=0, tiled=True)  23.8 us
    dynamic_slice x1, local copies, waits for them, and re-layouts, scattered(): kept = lax.dynamic_index_in_dim(halves, mine, 1, keepdims=False)  19 us
    reshape x1, local copies, waits for them, and re-layouts, scattered(): halves = term.reshape(1 << place, 2, (1 << below) * rows, columns)  17.9 us
  transfers between devices with their start and end apart: 11, of which 10 were waited for; matrix products, arithmetic and copies ran while one was open for 21% of the time, Pallas kernels for 8%

profile of v2, /device:TPU:6, one launch (start us, length us, event | category | flops | bytes accessed | tf_op | source)
XLA Modules:
  0.0 580.8 jit_solution(14802761415720816108)
XLA Ops:
  7.2 0.7 all-gather.2.cloned.1.call-update
  7.9 0.2 fusion.18
  8.1 0.7 iota_reduce_fusion
  8.9 0.1 reshape.149
  9.0 0.7 gather_fusion
  9.8 0.1 add.128
  9.9 0.1 eq.33
  10.0 0.1 add.130
  10.1 23.8 %all-gather.2.cloned.1.call-done = bf16[1024,5120]{1,0:T(8,128)(2,1)} async-done(((bf16[512,5120]{1,0:T(8,128)(2,1)}), bf16[1024,5120]{1,0:T(8,128)(2,1)}) %all-gather.2.cloned.1.call-update) | async-done | bytes 10485776 | tf_op jit(solution)/shard_map/all_gather | solution.py:167
  33.9 13.5 %fusion.15.g_ref = bf16[1024,768]{1,0:T(8,128)(2,1)S(1)} fusion(bf16[1024,5120]{1,0:T(8,128)(2,1)} %all-gather.2.cloned.1.call-done, bf16[1536,5120]{1,0:T(8,128)(2,1)} %param.11), kind=kOutput, calls=%fused_computation.26 | convolution fusion | flops 8053850112 | bytes 19922944 | tf_op jit(solution)/shard_map/dot_general | solution.py:18
  47.4 33.4 %shard_map.103 = (bf16[3,512,768]{2,1,0:T(8,128)(2,1)S(1)}, bf16[3,512,768]{2,1,0:T(8,128)(2,1)S(1)}, bf16[1024,768]{1,0:T(8,128)(2,1)S(1)}) custom-call(s32[8]{0:T(128)S(1)} %broadcast_minimum_fusion.starts, s32[32]{0:T(128)S(1)} %compare_convert_fusion.same, bf16[1024,1536]{1,0:T(8,128)(2,1)S(1)} %copy-done.8, bf16[1024,1536]{1,0:T(8,128)(2,1)S(1)} %copy-done.10, ...), custom_call_target="tpu_custom_call" | custom-call | flops 4026531840 | bytes 12582912 | tf_op jit(solution)/shard_map/pallas_call | solution.py:76
  80.8 1.4 copy-done.6
  82.2 15.3 %fusion.6 = bf16[5120,768]{0,1:T(8,128)(2,1)} fusion(bf16[1024,768]{1,0:T(8,128)(2,1)S(1)} %get-tuple-element.28, bf16[1024,5120]{1,0:T(8,128)(2,1)} %all-gather.2.cloned.1.call-done), kind=kOutput, calls=%fused_computation.11 | convolution fusion | flops 8060928000 | bytes 19922944 | tf_op jit(solution)/shard_map/dot_general | solution.py:18
  97.5 10.7 %copy.18 = bf16[5120,768]{1,0:T(8,128)(2,1)} copy(bf16[5120,768]{0,1:T(8,128)(2,1)} %fusion.6) | data formatting | bytes 15728640 | tf_op jit(solution)/shard_map/convert_element_type | solution.py:197
  108.2 4.3 dynamic-slice_bitcast_fusion
  112.5 0.6 collective-permute-start.2
  113.1 13.6 %fusion.12.g_ref = bf16[1024,768]{1,0:T(8,128)(2,1)S(1)} fusion(bf16[1024,5120]{1,0:T(8,128)(2,1)} %all-gather.2.cloned.1.call-done, bf16[1536,5120]{1,0:T(8,128)(2,1)} %param.11), kind=kOutput, calls=%fused_computation.25 | convolution fusion | flops 8053850112 | bytes 19922944 | tf_op jit(solution)/shard_map/dot_general | solution.py:18
  126.7 33.4 %shard_map.102 = (bf16[3,512,768]{2,1,0:T(8,128)(2,1)S(1)}, bf16[3,512,768]{2,1,0:T(8,128)(2,1)S(1)}, bf16[1024,768]{1,0:T(8,128)(2,1)S(1)}) custom-call(s32[8]{0:T(128)S(1)} %broadcast_minimum_fusion.starts, s32[32]{0:T(128)S(1)} %compare_convert_fusion.same, bf16[1024,1536]{1,0:T(8,128)(2,1)S(1)} %copy-done.9, bf16[1024,1536]{1,0:T(8,128)(2,1)S(1)} %copy-done.11, ...), custom_call_target="tpu_custom_call" | custom-call | flops 4026531840 | bytes 12582912 | tf_op jit(solution)/shard_map/pallas_call | solution.py:76
  160.1 1.4 copy-done.2
  161.5 14.3 %fusion.7 = bf16[5120,768]{0,1:T(8,128)(2,1)} fusion(bf16[1024,768]{1,0:T(8,128)(2,1)S(1)} %get-tuple-element.29, bf16[1024,5120]{1,0:T(8,128)(2,1)} %all-gather.2.cloned.1.call-done), kind=kOutput, calls=%fused_computation.12 | convolution fusion | flops 8060928000 | bytes 19922944 | tf_op jit(solution)/shard_map/dot_general | solution.py:18
  175.9 17.9 %reshape.139 = bf16[4,2,640,768]{2,1,0,3:T(2,128)(2,1)} reshape(bf16[5120,768]{0,1:T(8,128)(2,1)} %fusion.7) | data formatting | bytes 15728640 | tf_op jit(solution)/shard_map/reshape | solution.py:115
  193.8 19.0 %constant_dynamic-slice_fusion.2 = (bf16[4,1,640,768]{2,1,0,3:T(2,128)(2,1)}, bf16[4,1,640,768]{2,1,0,3:T(2,128)(2,1)}) fusion(bf16[4,2,640,768]{2,1,0,3:T(2,128)(2,1)} %reshape.139, s32[]{:T(128)S(6)} %select_n.75, s32[]{:T(128)S(6)} %select_n.76), kind=kLoop, calls=%fused_computation.34 | loop fusion | bytes 15728648 | tf_op jit(solution)/shard_map/jit(dynamic_index_in_dim)/dynamic_slice | solution.py:118
  212.8 16.1 %copy.23 = bf16[4,1,640,768]{3,2,0,1:T(8,128)(2,1)} copy(bf16[4,1,640,768]{2,1,0,3:T(2,128)(2,1)} %get-tuple-element.31) | data formatting | bytes 7864320
  229.0 0.2 collective-permute-start.6
  229.1 16.2 %copy.22 = bf16[4,1,640,768]{3,2,0,1:T(8,128)(2,1)} copy(bf16[4,1,640,768]{2,1,0,3:T(2,128)(2,1)} %get-tuple-element.30) | data formatting | bytes 7864320
  245.3 4.3 fusion.1
  249.6 1.4 dynamic-slice_bitcast_fusion.2
  251.0 1.8 collective-permute-start.3
  252.8 64.3 %collective-permute-done.6 = bf16[4,640,768]{2,1,0:T(8,128)(2,1)} collective-permute-done((bf16[4,640,768]{2,1,0:T(8,128)(2,1)}, bf16[4,640,768]{2,1,0:T(8,128)(2,1)}, u32[]{:S(2)}, u32[]{:S(2)}) %collective-permute-start.6) | collective-permute-done | bytes 3932192 | tf_op jit(solution)/shard_map/ppermute | solution.py:119
  317.1 3.1 fusion
  320.2 1.9 copy-done.15
  322.1 1.4 dynamic-slice_bitcast_fusion.1
  323.5 1.9 collective-permute-start.7
  325.4 2.4 collective-permute-start.1
  327.8 0.5 collective-permute-start
  328.3 29.8 %collective-permute-done.3 = bf16[4,320,768]{2,1,0:T(8,128)(2,1)} collective-permute-done((bf16[4,320,768]{2,1,0:T(8,128)(2,1)}, bf16[4,320,768]{2,1,0:T(8,128)(2,1)}, u32[]{:S(2)}, u32[]{:S(2)}) %collective-permute-start.3) | collective-permute-done | bytes 1966112 | tf_op jit(solution)/shard_map/ppermute | solution.py:119
  358.2 2.6 fusion.9
  360.8 1.6 collective-permute-start.4
  362.4 4.3 collective-permute-done.7
  366.7 2.1 fusion.8
  368.7 1.3 copy-done.19
  370.0 1.0 dynamic-slice_bitcast_fusion.3
  371.0 1.5 collective-permute-start.8
  372.5 78.8 %collective-permute-done.4 = bf16[2,320,768]{2,1,0:T(8,128)(2,1)} collective-permute-done((bf16[2,320,768]{2,1,0:T(8,128)(2,1)S(1)}, bf16[2,320,768]{2,1,0:T(8,128)(2,1)}, u32[]{:S(2)}, u32[]{:S(2)}) %collective-permute-start.4) | collective-permute-done | bytes 983072 | tf_op jit(solution)/shard_map/ppermute | solution.py:119
  451.3 1.7 fusion.11
  453.1 0.8 constant_dynamic-slice_fusion.3
  453.9 2.6 collective-permute-start.5
  456.5 16.0 %collective-permute-done.8 = bf16[2,320,768]{2,1,0:T(8,128)(2,1)} collective-permute-done((bf16[2,320,768]{2,1,0:T(8,128)(2,1)}, bf16[2,320,768]{2,1,0:T(8,128)(2,1)}, u32[]{:S(2)}, u32[]{:S(2)}) %collective-permute-start.8) | collective-permute-done | bytes 983072 | tf_op jit(solution)/shard_map/ppermute | solution.py:119
  472.5 1.4 fusion.10
  473.9 0.9 copy-done.21
  474.9 0.8 constant_dynamic-slice_fusion
  475.7 2.5 collective-permute-start.9
  478.2 0.6 dynamic_slice.53.moving
  478.8 21.9 %collective-permute-done.1.arrived_ref = bf16[3,512,768]{2,1,0:T(8,128)(2,1)} collective-permute-done((bf16[3,512,768]{2,1,0:T(8,128)(2,1)}, bf16[3,512,768]{2,1,0:T(8,128)(2,1)}, u32[]{:S(2)}, u32[]{:S(2)}) %collective-permute-start.1) | collective-permute-done | bytes 2359328 | tf_op jit(solution)/shard_map/ppermute | solution.py:196
  500.7 1.7 copy-done.5
  502.4 1.7 copy-done.7
  504.0 6.6 %shard_map.104 = (bf16[1024,1536]{1,0:T(8,128)(2,1)}, bf16[1024,1536]{1,0:T(8,128)(2,1)}, bf16[1024,1536]{1,0:T(8,128)(2,1)}) custom-call(s32[1]{0:T(128)} %dynamic_slice.53.moving, bf16[3,512,768]{2,1,0:T(8,128)(2,1)S(1)} %copy-done.5, bf16[3,512,768]{2,1,0:T(8,128)(2,1)S(1)} %copy-done.7, bf16[3,512,768]{2,1,0:T(8,128)(2,1)} %collective-permute-done.1.arrived_ref), custom_call_target="tpu_custom_call" | custom-call | bytes 11796480 | tf_op jit(solution)/shard_map/pallas_call | solution.py:148
  510.6 40.6 %collective-permute-done.arrived_ref = bf16[3,512,768]{2,1,0:T(8,128)(2,1)} collective-permute-done((bf16[3,512,768]{2,1,0:T(8,128)(2,1)}, bf16[3,512,768]{2,1,0:T(8,128)(2,1)}, u32[]{:S(2)}, u32[]{:S(2)}) %collective-permute-start) | collective-permute-done | bytes 2359328 | tf_op jit(solution)/shard_map/ppermute | solution.py:196
  551.3 6.7 %shard_map.105 = (bf16[1024,1536]{1,0:T(8,128)(2,1)}, bf16[1024,1536]{1,0:T(8,128)(2,1)}, bf16[1024,1536]{1,0:T(8,128)(2,1)}) custom-call(s32[1]{0:T(128)} %dynamic_slice.53.moving, bf16[3,512,768]{2,1,0:T(8,128)(2,1)S(1)} %get-tuple-element.18.lead_ref, ...), custom_call_target="tpu_custom_call", output_to_operand_aliasing={{0}: (4, {}), {1}: (5, {}), {2}: (6, {})} | custom-call | bytes 11796480 | tf_op jit(solution)/shard_map/pallas_call | solution.py:148
  558.0 3.8 collective-permute-done.5
  561.8 1.1 add_bitcast_fusion.1
  562.9 8.3 %collective-permute-done.9 = bf16[1,320,768]{2,1,0:T(8,128)(2,1)} collective-permute-done((bf16[1,320,768]{2,1,0:T(8,128)(2,1)}, bf16[1,320,768]{2,1,0:T(8,128)(2,1)}, u32[]{:S(2)}, u32[]{:S(2)}) %collective-permute-start.9) | collective-permute-done | bytes 491552 | tf_op jit(solution)/shard_map/ppermute | solution.py:119
  571.3 1.2 add_bitcast_fusion
  572.4 1.5 pad_maximum_fusion
  (51 shorter events, 0.5 us)
Async XLA Ops:
  7.2 0.8 copy-start
  7.2 26.7 %all-gather.2.cloned.1.call-start = ((), (), s32[]{:S(2)}) async-start(), calls=%async_computation | async-start | bytes 15728640 | tf_op jit(solution)/shard_map/all_gather | solution.py:167
  33.9 13.5 %copy-start.8 = (bf16[1024,1536]{1,0:T(8,128)(2,1)S(1)}, bf16[1024,1536]{1,0:T(8,128)(2,1)}, u32[]{:S(2)}) copy-start(bf16[1024,1536]{1,0:T(8,128)(2,1)} %q_ref.3) | copy-start | bytes 9437188
  33.9 13.5 %copy-start.10 = (bf16[1024,1536]{1,0:T(8,128)(2,1)S(1)}, bf16[1024,1536]{1,0:T(8,128)(2,1)}, u32[]{:S(2)}) copy-start(bf16[1024,1536]{1,0:T(8,128)(2,1)} %k_ref.3) | copy-start | bytes 9437188
  33.9 13.5 %copy-start.12 = (bf16[1024,1536]{1,0:T(8,128)(2,1)S(1)}, bf16[1024,1536]{1,0:T(8,128)(2,1)}, u32[]{:S(2)}) copy-start(bf16[1024,1536]{1,0:T(8,128)(2,1)} %v_ref.3) | copy-start | bytes 9437188
  80.8 1.4 copy-start.6
  82.2 15.3 %copy-start.4 = (bf16[3,512,768]{2,1,0:T(8,128)(2,1)}, bf16[3,512,768]{2,1,0:T(8,128)(2,1)S(1)}, u32[]{:S(2)}) copy-start(bf16[3,512,768]{2,1,0:T(8,128)(2,1)S(1)} %get-tuple-element.20.lead_ref) | copy-start | bytes 7077892
  112.5 14.2 %copy-start.9 = (bf16[1024,1536]{1,0:T(8,128)(2,1)S(1)}, bf16[1024,1536]{1,0:T(8,128)(2,1)}, u32[]{:S(2)}) copy-start(bf16[1024,1536]{1,0:T(8,128)(2,1)} %q_ref.3) | copy-start | bytes 9437188
  112.5 14.2 %copy-start.11 = (bf16[1024,1536]{1,0:T(8,128)(2,1)S(1)}, bf16[1024,1536]{1,0:T(8,128)(2,1)}, u32[]{:S(2)}) copy-start(bf16[1024,1536]{1,0:T(8,128)(2,1)} %k_ref.3) | copy-start | bytes 9437188
  112.5 14.2 %copy-start.13 = (bf16[1024,1536]{1,0:T(8,128)(2,1)S(1)}, bf16[1024,1536]{1,0:T(8,128)(2,1)}, u32[]{:S(2)}) copy-start(bf16[1024,1536]{1,0:T(8,128)(2,1)} %v_ref.3) | copy-start | bytes 9437188
  112.5 132.8 %collective-permute-start.2 = (bf16[8,320,768]{2,1,0:T(8,128)(2,1)}, bf16[8,320,768]{2,1,0:T(8,128)(2,1)}, u32[]{:S(2)}, u32[]{:S(2)}) collective-permute-start(bf16[8,320,768]{2,1,0:T(8,128)(2,1)} %dynamic-slice_bitcast_fusion), channel_id=1, source_target_pairs={{0,2},{2,0},{4,6},{6,4},{8,10},{10,8},{12,14},{14,12},{16,18},{18,... | collective-permute-start | bytes 11796488 | tf_op jit(solution)/shard_map/ppermute | solution.py:119
  160.1 1.4 copy-start.2
  229.0 88.1 %collective-permute-start.6 = (bf16[4,640,768]{2,1,0:T(8,128)(2,1)}, bf16[4,640,768]{2,1,0:T(8,128)(2,1)}, u32[]{:S(2)}, u32[]{:S(2)}) collective-permute-start(bf16[4,640,768]{2,1,0:T(8,128)(2,1)} %bitcast.68), channel_id=1, source_target_pairs={{0,4},{2,6},{4,0},{6,2},{8,12},{10,14},{12,8},{14,10},{16,20},{18,... | collective-permute-start | bytes 11796488 | tf_op jit(solution)/shard_map/ppermute | solution.py:119
  249.6 70.7 %copy-start.14 = (bf16[8,320,768]{2,1,0:T(8,128)(2,1)}, bf16[8,320,768]{2,1,0:T(8,128)(2,1)S(1)}, u32[]{:S(2)}) copy-start(bf16[8,320,768]{2,1,0:T(8,128)(2,1)S(1)} %fusion.1) | copy-start | bytes 11796484
  249.6 67.5 %copy-start.17 = (bf16[4,1,640,768]{3,2,0,1:T(8,128)(2,1)S(1)}, bf16[4,1,640,768]{3,2,0,1:T(8,128)(2,1)}, u32[]{:S(2)}) copy-start(bf16[4,1,640,768]{3,2,0,1:T(8,128)(2,1)} %copy.22) | copy-start | bytes 11796484
  251.0 107.2 %collective-permute-start.3 = (bf16[4,320,768]{2,1,0:T(8,128)(2,1)}, bf16[4,320,768]{2,1,0:T(8,128)(2,1)}, u32[]{:S(2)}, u32[]{:S(2)}) collective-permute-start(bf16[4,320,768]{2,1,0:T(8,128)(2,1)} %dynamic-slice_bitcast_fusion.2), channel_id=1, source_target_pairs={{0,4},{2,6},{4,0},{6,2},{8,12},{10,14},{12,8},{14,10},{16,20},{18,... | collective-permute-start | bytes 5898248 | tf_op jit(solution)/shard_map/ppermute | solution.py:119
  320.2 1.9 copy-start.15
  323.5 43.1 %collective-permute-start.7 = (bf16[4,320,768]{2,1,0:T(8,128)(2,1)}, bf16[4,320,768]{2,1,0:T(8,128)(2,1)}, u32[]{:S(2)}, u32[]{:S(2)}) collective-permute-start(bf16[4,320,768]{2,1,0:T(8,128)(2,1)} %dynamic-slice_bitcast_fusion.1), channel_id=1, source_target_pairs={{0,2},{2,0},{4,6},{6,4},{8,10},{10,8},{12,14},{14,12},{16,18},{18,... | collective-permute-start | bytes 5898248 | tf_op jit(solution)/shard_map/ppermute | solution.py:119
  325.4 175.3 %collective-permute-start.1 = (bf16[3,512,768]{2,1,0:T(8,128)(2,1)}, bf16[3,512,768]{2,1,0:T(8,128)(2,1)}, u32[]{:S(2)}, u32[]{:S(2)}) collective-permute-start(bf16[3,512,768]{2,1,0:T(8,128)(2,1)} %copy-done.6), channel_id=1, source_target_pairs={{0,16},{2,18},{4,20},{6,22},{8,24},{10,26},{12,28},{14,30},{16,0},... | collective-permute-start | bytes 7077896 | tf_op jit(solution)/shard_map/ppermute | solution.py:196
  327.8 38.9 %copy-start.16 = (bf16[4,640,768]{2,1,0:T(8,128)(2,1)S(1)}, bf16[4,640,768]{2,1,0:T(8,128)(2,1)}, u32[]{:S(2)}) copy-start(bf16[4,640,768]{2,1,0:T(8,128)(2,1)} %copy-done.15) | copy-start | bytes 11796484
  327.8 223.5 %collective-permute-start = (bf16[3,512,768]{2,1,0:T(8,128)(2,1)}, bf16[3,512,768]{2,1,0:T(8,128)(2,1)}, u32[]{:S(2)}, u32[]{:S(2)}) collective-permute-start(bf16[3,512,768]{2,1,0:T(8,128)(2,1)} %copy-done.2), channel_id=1, source_target_pairs={{0,16},{2,18},{4,20},{6,22},{8,24},{10,26},{12,28},{14,30},{16,0},... | collective-permute-start | bytes 7077896 | tf_op jit(solution)/shard_map/ppermute | solution.py:196
  360.8 8.0 %copy-start.18 = (bf16[4,320,768]{2,1,0:T(8,128)(2,1)}, bf16[4,320,768]{2,1,0:T(8,128)(2,1)S(1)}, u32[]{:S(2)}) copy-start(bf16[4,320,768]{2,1,0:T(8,128)(2,1)S(1)} %fusion.9) | copy-start | bytes 5898244
  360.8 90.5 %collective-permute-start.4 = (bf16[2,320,768]{2,1,0:T(8,128)(2,1)S(1)}, bf16[2,320,768]{2,1,0:T(8,128)(2,1)}, u32[]{:S(2)}, u32[]{:S(2)}) collective-permute-start(bf16[2,320,768]{2,1,0:T(8,128)(2,1)S(1)} %dynamic-slice_bitcast_fusion.4), channel_id=1, source_target_pairs={{0,8},{2,10},{4,12},{6,14},{8,0},{10,2},{12,4},{14,6},{16,24},{18,... | collective-permute-start | bytes 2949128 | tf_op jit(solution)/shard_map/ppermute | solution.py:119
  368.7 1.3 copy-start.19
  371.0 101.5 %collective-permute-start.8 = (bf16[2,320,768]{2,1,0:T(8,128)(2,1)}, bf16[2,320,768]{2,1,0:T(8,128)(2,1)}, u32[]{:S(2)}, u32[]{:S(2)}) collective-permute-start(bf16[2,320,768]{2,1,0:T(8,128)(2,1)} %dynamic-slice_bitcast_fusion.3), channel_id=1, source_target_pairs={{0,8},{2,10},{4,12},{6,14},{8,0},{10,2},{12,4},{14,6},{16,24},{18,... | collective-permute-start | bytes 2949128 | tf_op jit(solution)/shard_map/ppermute | solution.py:119
  372.5 100.0 %copy-start.20 = (bf16[4,320,768]{2,1,0:T(8,128)(2,1)S(1)}, bf16[4,320,768]{2,1,0:T(8,128)(2,1)}, u32[]{:S(2)}) copy-start(bf16[4,320,768]{2,1,0:T(8,128)(2,1)} %copy-done.19) | copy-start | bytes 5898244
  372.5 105.6 %copy-start.23 = (s32[16]{0:T(128)S(1)}, s32[16]{0:T(128)}, u32[]{:S(2)}) copy-start(s32[16]{0:T(128)} %param.13) | copy-start | bytes 196
  453.9 107.9 %collective-permute-start.5 = (bf16[1,320,768]{2,1,0:T(8,128)(2,1)}, bf16[1,320,768]{2,1,0:T(8,128)(2,1)}, u32[]{:S(2)}, u32[]{:S(2)}) collective-permute-start(bf16[1,320,768]{2,1,0:T(8,128)(2,1)} %constant_dynamic-slice_fusion.3), channel_id=1, source_target_pairs={{0,16},{2,18},{4,20},{6,22},{8,24},{10,26},{12,28},{14,30},{16,0},... | collective-permute-start | bytes 1474568 | tf_op jit(solution)/shard_map/ppermute | solution.py:119
  473.9 0.9 copy-start.21
  475.7 95.5 %collective-permute-start.9 = (bf16[1,320,768]{2,1,0:T(8,128)(2,1)}, bf16[1,320,768]{2,1,0:T(8,128)(2,1)}, u32[]{:S(2)}, u32[]{:S(2)}) collective-permute-start(bf16[1,320,768]{2,1,0:T(8,128)(2,1)} %constant_dynamic-slice_fusion), channel_id=1, source_target_pairs={{0,16},{2,18},{4,20},{6,22},{8,24},{10,26},{12,28},{14,30},{16,0},... | collective-permute-start | bytes 1474568 | tf_op jit(solution)/shard_map/ppermute | solution.py:119
  478.8 72.4 %copy-start.3 = (bf16[3,512,768]{2,1,0:T(8,128)(2,1)S(1)}, bf16[3,512,768]{2,1,0:T(8,128)(2,1)}, u32[]{:S(2)}) copy-start(bf16[3,512,768]{2,1,0:T(8,128)(2,1)} %copy-done.2) | copy-start | bytes 7077892
  500.7 1.7 copy-start.5
  502.4 1.7 copy-start.7
  551.3 20.0 %copy-start.22 = (bf16[2,320,768]{2,1,0:T(8,128)(2,1)S(1)}, bf16[2,320,768]{2,1,0:T(8,128)(2,1)}, u32[]{:S(2)}) copy-start(bf16[2,320,768]{2,1,0:T(8,128)(2,1)} %copy-done.21) | copy-start | bytes 2949124
  551.3 22.7 %copy-start.1 = (s32[16,8]{0,1:T(8,128)S(1)}, s32[16,8]{0,1:T(8,128)}, u32[]{:S(2)}) copy-start(s32[16,8]{0,1:T(8,128)} %param.12) | copy-start | bytes 1540
Sparse Core Ops, SparseCore 0:
  9.6 24.2 all-gather.1

commit v3 on v2

--- a/solution.py
+++ b/solution.py
@@ -103,12 +103,14 @@
     )(starts, same, query, key_rows, value, gradient)
 
 
-def scattered(term, order):
+def scattered(term, moved, tie):
     replicas = lax.axis_size("dp")
     position = lax.axis_index("dp")
     rows, columns = term.shape[0] // replicas, term.shape[1]
     remaining = list(reversed(range(replicas.bit_length() - 1)))
-    for bit in order:
+    for bit in range(replicas.bit_length() - 1):
+        if bit == tie:
+            term, moved = lax.optimization_barrier((term, moved))
         place = remaining.index(bit)
         remaining.pop(place)
         below = len(remaining) - place
@@ -121,7 +123,7 @@
         term = total.reshape(-1, columns)
         if remaining:
             term = term.astype(jnp.bfloat16)
-    return term
+    return term, moved
 
 
 def settle_kernel(blocks, moving, lead_ref, trail_ref, arrived_ref, *refs):
@@ -181,8 +183,6 @@
     near = jnp.take(ids, starts[:, None] + jnp.arange(window, dtype=jnp.int32)[None, :])
     same = (near == ids[:, None]).astype(jnp.int32).reshape(-1)
     pairs = [(i, (i + halfway) % replicas) for i in range(replicas)]
-    upward = list(range(replicas.bit_length() - 1))
-    orders = [upward, [1, 0] + upward[2:]]
 
     moves, weight_parts = [], []
     for group in range(groups):
@@ -193,9 +193,12 @@
         lead, trail, head_output = attend(
             queries, keys, values, head_gradient, starts, same, group * each, each, window, trailing
         )
-        moves.append((lead, trail, lax.ppermute(trail, "dp", pairs)))
+        if moves:
+            head_output, moves[-1][2] = lax.optimization_barrier((head_output, moves[-1][2]))
+        moves.append([lead, trail, lax.ppermute(trail, "dp", pairs)])
         term = (contract(full_gradient, head_output, ((0,), (0,))) / replicas).astype(jnp.bfloat16)
-        weight_parts.append(scattered(term, orders[group % 2]))
+        part, moves[-1][2] = scattered(term, moves[-1][2], 2 if group == groups - 1 else None)
+        weight_parts.append(part)
 
     settled = ()
     for group, (lead, trail, arrived) in enumerate(moves):

time: 584 us -> 460 us (0.79)
  waiting for transfers between devices: 292 us -> 219 us
  local copies, waits for them, and re-layouts: 102 us -> 52.5 us
    ppermute x8, waiting for transfers between devices: 205 us -> 143 us  [scattered(): lax.ppermute(sent, 'dp', [(i, i ^ 1 << bit) for i in range(replicas)])]
    unnamed x50 -> x56, local copies, waits for them, and re-layouts: 42.6 us -> 13.8 us
    dynamic_slice x1 -> x0, local copies, waits for them, and re-layouts: 19 us -> none  [scattered(): kept = lax.dynamic_index_in_dim(halves, mine, 1, keepdims=False)]
    reshape x1 -> x0, local copies, waits for them, and re-layouts: 17.9 us -> none  [scattered(): halves = term.reshape(1 << place, 2, (1 << below) * rows, columns)]
    ppermute x2, waiting for transfers between devices: 62.5 us -> 51.6 us  [shards(): moves.append([lead, trail, lax.ppermute(trail, 'dp', pairs)])]
    convert_element_type x1 -> x2, local copies, waits for them, and re-layouts: 10.7 us -> 21.4 us  [shards(): (contract(full_gradient, head_output, ((0,), (0,))) / replicas).astype(jn...]
    squeeze x7 -> x8, local copies, waits for them, and re-layouts: 9.88 us -> 15.4 us  [scattered(): sent = lax.dynamic_index_in_dim(halves, 1 - mine, 1, keepdims=False)]
  transfers between devices with their start and end apart: 11 -> 11, of which waited for: 10 -> 6; matrix products, arithmetic and copies ran while one was open for 21% -> 15% of each run, Pallas kernels for 8% -> 10%
where the time goes in v3:
time: 460 us; the launch traced here: 457 us
  waiting for transfers between devices  219 us (48%)
  Pallas kernels  78.3 us (17%)
  matrix products  57.6 us (13%)
  local copies, waits for them, and re-layouts  52.5 us (11%)
  other arithmetic  20 us (4%)
  starting transfers between devices  15.2 us (3%)
  between operations  14.3 us (3%)
    ppermute x8, waiting for transfers between devices, scattered(): lax.ppermute(sent, 'dp', [(i, i ^ 1 << bit) for i in range(replicas)])  143 us
    pallas_call x2, Pallas kernels, attend(): pl.pallas_call(functools.partial(attend_kernel, window), out_shape=(jax.S...  66.8 us
    dot_general x4, matrix products, contract(): lax.dot_general(a, b, (dims, ((), ())), preferred_element_type=jnp.float32)  57.6 us
    ppermute x2, waiting for transfers between devices, shards(): moves.append([lead, trail, lax.ppermute(trail, 'dp', pairs)])  51.6 us
    all_gather x1, waiting for transfers between devices, shards(): full_gradient = lax.all_gather(out_gradient, 'tensor', axis=0, tiled=True)  23.8 us
    convert_element_type x2, local copies, waits for them, and re-layouts, shards(): (contract(full_gradient, head_output, ((0,), (0,))) / replicas).astype(jn...  21.4 us
    squeeze x8, local copies, waits for them, and re-layouts, scattered(): sent = lax.dynamic_index_in_dim(halves, 1 - mine, 1, keepdims=False)  15.4 us
    convert_element_type x6, other arithmetic, scattered(): term = term.astype(jnp.bfloat16)  15.4 us
  transfers between devices with their start and end apart: 11, of which 6 were waited for; matrix products, arithmetic and copies ran while one was open for 15% of the time, Pallas kernels for 10%

profile of v3, /device:TPU:6, one launch (start us, length us, event | category | flops | bytes accessed | tf_op | source)
XLA Modules:
  0.0 456.6 jit_solution(16549428168882691225)
XLA Ops:
  7.2 0.0 all-gather.2.cloned.1.call-start
  7.2 0.7 all-gather.2.cloned.1.call-update
  7.9 0.2 fusion.18
  8.1 0.7 iota_reduce_fusion
  8.8 0.1 compare_select_fusion
  8.9 0.1 reshape.151
  9.0 0.7 gather_fusion
  9.7 0.1 add.126
  9.8 0.1 add.127
  9.8 0.1 eq.32
  9.9 0.1 eq.33
  10.0 0.1 add.129
  10.1 23.8 %all-gather.2.cloned.1.call-done = bf16[1024,5120]{1,0:T(8,128)(2,1)} async-done(((bf16[512,5120]{1,0:T(8,128)(2,1)}), bf16[1024,5120]{1,0:T(8,128)(2,1)}) %all-gather.2.cloned.1.call-update) | async-done | bytes 10485776 | tf_op jit(solution)/shard_map/all_gather | solution.py:169
  33.9 13.5 %fusion.15.g_ref = bf16[1024,768]{1,0:T(8,128)(2,1)S(1)} fusion(bf16[1024,5120]{1,0:T(8,128)(2,1)} %all-gather.2.cloned.1.call-done, bf16[1536,5120]{1,0:T(8,128)(2,1)} %param.11), kind=kOutput, calls=%fused_computation.27 | convolution fusion | flops 8053850112 | bytes 19922944 | tf_op jit(solution)/shard_map/dot_general | solution.py:18
  47.4 33.4 %shard_map.103 = (bf16[3,512,768]{2,1,0:T(8,128)(2,1)S(1)}, bf16[3,512,768]{2,1,0:T(8,128)(2,1)S(1)}, bf16[1024,768]{1,0:T(8,128)(2,1)S(1)}) custom-call(s32[8]{0:T(128)S(1)} %broadcast_minimum_fusion.starts, s32[32]{0:T(128)S(1)} %compare_convert_fusion.same, bf16[1024,1536]{1,0:T(8,128)(2,1)S(1)} %copy-done.11, bf16[1024,1536]{1,0:T(8,128)(2,1)S(1)} %copy-done.13, ...), custom_call_target="tpu_custom_call" | custom-call | flops 4026531840 | bytes 12582912 | tf_op jit(solution)/shard_map/pallas_call | solution.py:76
  80.8 1.4 copy-done.6
  82.2 15.3 %fusion.7 = bf16[5120,768]{0,1:T(8,128)(2,1)} fusion(bf16[1024,768]{1,0:T(8,128)(2,1)S(1)} %get-tuple-element.36, bf16[1024,5120]{1,0:T(8,128)(2,1)} %all-gather.2.cloned.1.call-done), kind=kOutput, calls=%fused_computation.12 | convolution fusion | flops 8060928000 | bytes 19922944 | tf_op jit(solution)/shard_map/dot_general | solution.py:18
  97.5 10.7 %copy.18 = bf16[5120,768]{1,0:T(8,128)(2,1)} copy(bf16[5120,768]{0,1:T(8,128)(2,1)} %fusion.7) | data formatting | bytes 15728640 | tf_op jit(solution)/shard_map/convert_element_type | solution.py:199
  108.2 4.4 dynamic-slice_bitcast_fusion
  112.6 0.6 collective-permute-start.4
  113.2 2.5 collective-permute-start
  115.6 14.5 %fusion.12.g_ref = bf16[1024,768]{1,0:T(8,128)(2,1)} fusion(bf16[1024,5120]{1,0:T(8,128)(2,1)} %all-gather.2.cloned.1.call-done, bf16[1536,5120]{1,0:T(8,128)(2,1)} %param.11), kind=kOutput, calls=%fused_computation.26 | convolution fusion | flops 8053850112 | bytes 19922944 | tf_op jit(solution)/shard_map/dot_general | solution.py:18
  130.1 1.4 copy-done.17
  131.5 33.4 %shard_map.102 = (bf16[3,512,768]{2,1,0:T(8,128)(2,1)S(1)}, bf16[3,512,768]{2,1,0:T(8,128)(2,1)S(1)}, bf16[1024,768]{1,0:T(8,128)(2,1)S(1)}) custom-call(s32[8]{0:T(128)S(1)} %broadcast_minimum_fusion.starts, s32[32]{0:T(128)S(1)} %compare_convert_fusion.same, bf16[1024,1536]{1,0:T(8,128)(2,1)S(1)} %copy-done.12, bf16[1024,1536]{1,0:T(8,128)(2,1)S(1)} %copy-done.14, ...), custom_call_target="tpu_custom_call" | custom-call | flops 4026531840 | bytes 12582912 | tf_op jit(solution)/shard_map/pallas_call | solution.py:76
  164.9 1.4 copy-done.2
  166.3 51.6 %collective-permute-done.arrived_ref = bf16[3,512,768]{2,1,0:T(8,128)(2,1)S(1)} collective-permute-done((bf16[3,512,768]{2,1,0:T(8,128)(2,1)S(1)}, bf16[3,512,768]{2,1,0:T(8,128)(2,1)S(1)}, u32[]{:S(2)}, u32[]{:S(2)}) %collective-permute-start) | collective-permute-done | bytes 2359328 | tf_op jit(solution)/shard_map/ppermute | solution.py:198
  217.9 1.4 copy-done.9
  219.3 14.4 %fusion.6 = bf16[5120,768]{0,1:T(8,128)(2,1)} fusion(bf16[1024,768]{1,0:T(8,128)(2,1)S(1)} %get-tuple-element.26, bf16[1024,5120]{1,0:T(8,128)(2,1)} %all-gather.2.cloned.1.call-done), kind=kOutput, calls=%fused_computation.11 | convolution fusion | flops 8060928000 | bytes 19922944 | tf_op jit(solution)/shard_map/dot_general | solution.py:18
  233.7 10.7 %copy.17 = bf16[5120,768]{1,0:T(8,128)(2,1)} copy(bf16[5120,768]{0,1:T(8,128)(2,1)} %fusion.6) | data formatting | bytes 15728640 | tf_op jit(solution)/shard_map/convert_element_type | solution.py:199
  244.3 4.3 dynamic-slice_bitcast_fusion.1
  248.6 1.5 collective-permute-start.1
  250.1 4.4 fusion
  254.5 1.4 dynamic-slice_bitcast_fusion.2
  256.0 0.5 collective-permute-start.5
  256.5 78.5 %collective-permute-done.1 = bf16[8,320,768]{2,1,0:T(8,128)(2,1)} collective-permute-done((bf16[8,320,768]{2,1,0:T(8,128)(2,1)}, bf16[8,320,768]{2,1,0:T(8,128)(2,1)}, u32[]{:S(2)}, u32[]{:S(2)}) %collective-permute-start.1) | collective-permute-done | bytes 3932192 | tf_op jit(solution)/shard_map/ppermute | solution.py:121
  335.0 3.1 fusion.1
  338.2 1.9 copy-done.20
  340.0 1.4 dynamic-slice_bitcast_fusion.3
  341.4 0.3 collective-permute-start.2
  341.8 2.7 fusion.8
  344.5 1.2 dynamic-slice_bitcast_fusion.5
  345.7 1.6 collective-permute-start.6
  347.2 37.5 %collective-permute-done.2 = bf16[4,320,768]{2,1,0:T(8,128)(2,1)} collective-permute-done((bf16[4,320,768]{2,1,0:T(8,128)(2,1)}, bf16[4,320,768]{2,1,0:T(8,128)(2,1)}, u32[]{:S(2)}, u32[]{:S(2)}) %collective-permute-start.2) | collective-permute-done | bytes 1966112 | tf_op jit(solution)/shard_map/ppermute | solution.py:121
  384.7 2.1 fusion.9
  386.8 1.3 copy-done.23
  388.1 1.0 dynamic-slice_bitcast_fusion.4
  389.1 2.2 collective-permute-start.8
  391.3 1.6 fusion.11
  392.9 0.9 constant_dynamic-slice_fusion.1
  393.8 3.4 collective-permute-start.7
  397.2 25.2 %collective-permute-done.8 = bf16[2,320,768]{2,1,0:T(8,128)(2,1)} collective-permute-done((bf16[2,320,768]{2,1,0:T(8,128)(2,1)}, bf16[2,320,768]{2,1,0:T(8,128)(2,1)}, u32[]{:S(2)}, u32[]{:S(2)}) %collective-permute-start.8) | collective-permute-done | bytes 983072 | tf_op jit(solution)/shard_map/ppermute | solution.py:121
  422.3 1.4 fusion.10
  423.8 0.8 constant_dynamic-slice_fusion
  424.6 2.6 collective-permute-start.9
  427.3 0.6 dynamic_slice.52.moving
  427.9 1.7 copy-done.5
  429.5 1.7 copy-done.8
  431.2 1.7 copy-done.10
  432.9 5.0 %shard_map.104 = (bf16[1024,1536]{1,0:T(8,128)(2,1)}, bf16[1024,1536]{1,0:T(8,128)(2,1)}, bf16[1024,1536]{1,0:T(8,128)(2,1)}) custom-call(s32[1]{0:T(128)} %dynamic_slice.52.moving, bf16[3,512,768]{2,1,0:T(8,128)(2,1)S(1)} %copy-done.5, bf16[3,512,768]{2,1,0:T(8,128)(2,1)S(1)} %copy-done.8, bf16[3,512,768]{2,1,0:T(8,128)(2,1)S(1)} %copy-done.10), custom_call_target="tpu_custom_call" | custom-call | bytes 11796480 | tf_op jit(solution)/shard_map/pallas_call | solution.py:150
  437.9 1.1 add_bitcast_fusion.1
  439.0 6.6 %shard_map.105 = (bf16[1024,1536]{1,0:T(8,128)(2,1)}, bf16[1024,1536]{1,0:T(8,128)(2,1)}, bf16[1024,1536]{1,0:T(8,128)(2,1)}) custom-call(s32[1]{0:T(128)} %dynamic_slice.52.moving, bf16[3,512,768]{2,1,0:T(8,128)(2,1)S(1)} %get-tuple-element.22.lead_ref, ...), custom_call_target="tpu_custom_call", output_to_operand_aliasing={{0}: (4, {}), {1}: (5, {}), {2}: (6, {})} | custom-call | bytes 11796480 | tf_op jit(solution)/shard_map/pallas_call | solution.py:150
  445.6 1.5 collective-permute-done.9
  447.1 1.1 add_bitcast_fusion
  448.3 1.5 pad_maximum_fusion
  (57 shorter events, 0.2 us)
Async XLA Ops:
  7.2 0.8 copy-start
  7.2 26.7 %all-gather.2.cloned.1.call-start = ((), (), s32[]{:S(2)}) async-start(), calls=%async_computation | async-start | bytes 15728640 | tf_op jit(solution)/shard_map/all_gather | solution.py:169
  33.9 13.5 %copy-start.11 = (bf16[1024,1536]{1,0:T(8,128)(2,1)S(1)}, bf16[1024,1536]{1,0:T(8,128)(2,1)}, u32[]{:S(2)}) copy-start(bf16[1024,1536]{1,0:T(8,128)(2,1)} %q_ref.3) | copy-start | bytes 9437188
  33.9 13.5 %copy-start.13 = (bf16[1024,1536]{1,0:T(8,128)(2,1)S(1)}, bf16[1024,1536]{1,0:T(8,128)(2,1)}, u32[]{:S(2)}) copy-start(bf16[1024,1536]{1,0:T(8,128)(2,1)} %k_ref.3) | copy-start | bytes 9437188
  33.9 13.5 %copy-start.15 = (bf16[1024,1536]{1,0:T(8,128)(2,1)S(1)}, bf16[1024,1536]{1,0:T(8,128)(2,1)}, u32[]{:S(2)}) copy-start(bf16[1024,1536]{1,0:T(8,128)(2,1)} %v_ref.3) | copy-start | bytes 9437188
  80.8 1.4 copy-start.6
  82.2 15.3 %copy-start.4 = (bf16[3,512,768]{2,1,0:T(8,128)(2,1)}, bf16[3,512,768]{2,1,0:T(8,128)(2,1)S(1)}, u32[]{:S(2)}) copy-start(bf16[3,512,768]{2,1,0:T(8,128)(2,1)S(1)} %get-tuple-element.28.lead_ref) | copy-start | bytes 7077892
  108.2 4.9 %copy-start.7 = (bf16[3,512,768]{2,1,0:T(8,128)(2,1)S(1)}, bf16[3,512,768]{2,1,0:T(8,128)(2,1)}, u32[]{:S(2)}) copy-start(bf16[3,512,768]{2,1,0:T(8,128)(2,1)} %copy-done.6) | copy-start | bytes 7077892
  112.6 137.5 %collective-permute-start.4 = (bf16[8,320,768]{2,1,0:T(8,128)(2,1)}, bf16[8,320,768]{2,1,0:T(8,128)(2,1)}, u32[]{:S(2)}, u32[]{:S(2)}) collective-permute-start(bf16[8,320,768]{2,1,0:T(8,128)(2,1)} %dynamic-slice_bitcast_fusion), channel_id=1, source_target_pairs={{0,2},{2,0},{4,6},{6,4},{8,10},{10,8},{12,14},{14,12},{16,18},{18,... | collective-permute-start | bytes 11796488 | tf_op jit(solution)/shard_map/ppermute | solution.py:121
  113.2 16.9 %copy-start.12 = (bf16[1024,1536]{1,0:T(8,128)(2,1)S(1)}, bf16[1024,1536]{1,0:T(8,128)(2,1)}, u32[]{:S(2)}) copy-start(bf16[1024,1536]{1,0:T(8,128)(2,1)} %q_ref.3) | copy-start | bytes 9437188
  113.2 16.9 %copy-start.14 = (bf16[1024,1536]{1,0:T(8,128)(2,1)S(1)}, bf16[1024,1536]{1,0:T(8,128)(2,1)}, u32[]{:S(2)}) copy-start(bf16[1024,1536]{1,0:T(8,128)(2,1)} %k_ref.3) | copy-start | bytes 9437188
  113.2 16.9 %copy-start.16 = (bf16[1024,1536]{1,0:T(8,128)(2,1)S(1)}, bf16[1024,1536]{1,0:T(8,128)(2,1)}, u32[]{:S(2)}) copy-start(bf16[1024,1536]{1,0:T(8,128)(2,1)} %v_ref.3) | copy-start | bytes 9437188
  113.2 104.7 %collective-permute-start = (bf16[3,512,768]{2,1,0:T(8,128)(2,1)S(1)}, bf16[3,512,768]{2,1,0:T(8,128)(2,1)S(1)}, u32[]{:S(2)}, u32[]{:S(2)}) collective-permute-start(bf16[3,512,768]{2,1,0:T(8,128)(2,1)S(1)} %copy-done.7), channel_id=1, source_target_pairs={{0,16},{2,18},{4,20},{6,22},{8,24},{10,26},{12,28},{14,30},{16,0},... | collective-permute-start | bytes 7077896 | tf_op jit(solution)/shard_map/ppermute | solution.py:198
  130.1 1.4 copy-start.17
  164.9 1.4 copy-start.2
  217.9 1.4 copy-start.9
  248.6 86.4 %collective-permute-start.1 = (bf16[8,320,768]{2,1,0:T(8,128)(2,1)}, bf16[8,320,768]{2,1,0:T(8,128)(2,1)}, u32[]{:S(2)}, u32[]{:S(2)}) collective-permute-start(bf16[8,320,768]{2,1,0:T(8,128)(2,1)} %dynamic-slice_bitcast_fusion.1), channel_id=1, source_target_pairs={{0,2},{2,0},{4,6},{6,4},{8,10},{10,8},{12,14},{14,12},{16,18},{18,... | collective-permute-start | bytes 11796488 | tf_op jit(solution)/shard_map/ppermute | solution.py:121
  250.1 136.7 %collective-permute-start.3 = (bf16[3,512,768]{2,1,0:T(8,128)(2,1)}, bf16[3,512,768]{2,1,0:T(8,128)(2,1)}, u32[]{:S(2)}, u32[]{:S(2)}) collective-permute-start(bf16[3,512,768]{2,1,0:T(8,128)(2,1)} %copy-done.2), channel_id=1, source_target_pairs={{0,16},{2,18},{4,20},{6,22},{8,24},{10,26},{12,28},{14,30},{16,0},... | collective-permute-start | bytes 7077896 | tf_op jit(solution)/shard_map/ppermute | solution.py:198
  250.1 84.9 %copy-start.18 = (bf16[5120,768]{1,0:T(8,128)(2,1)S(1)}, bf16[5120,768]{1,0:T(8,128)(2,1)}, u32[]{:S(2)}) copy-start(bf16[5120,768]{1,0:T(8,128)(2,1)} %copy.17) | copy-start | bytes 23592964
  254.5 83.6 %copy-start.19 = (bf16[8,320,768]{2,1,0:T(8,128)(2,1)}, bf16[8,320,768]{2,1,0:T(8,128)(2,1)S(1)}, u32[]{:S(2)}) copy-start(bf16[8,320,768]{2,1,0:T(8,128)(2,1)S(1)} %fusion) | copy-start | bytes 11796484
  256.0 85.8 %collective-permute-start.5 = (bf16[4,320,768]{2,1,0:T(8,128)(2,1)}, bf16[4,320,768]{2,1,0:T(8,128)(2,1)}, u32[]{:S(2)}, u32[]{:S(2)}) collective-permute-start(bf16[4,320,768]{2,1,0:T(8,128)(2,1)} %dynamic-slice_bitcast_fusion.2), channel_id=1, source_target_pairs={{0,4},{2,6},{4,0},{6,2},{8,12},{10,14},{12,8},{14,10},{16,20},{18,... | collective-permute-start | bytes 5898248 | tf_op jit(solution)/shard_map/ppermute | solution.py:121
  338.1 1.9 copy-start.20
  341.4 43.3 %collective-permute-start.2 = (bf16[4,320,768]{2,1,0:T(8,128)(2,1)}, bf16[4,320,768]{2,1,0:T(8,128)(2,1)}, u32[]{:S(2)}, u32[]{:S(2)}) collective-permute-start(bf16[4,320,768]{2,1,0:T(8,128)(2,1)} %dynamic-slice_bitcast_fusion.3), channel_id=1, source_target_pairs={{0,4},{2,6},{4,0},{6,2},{8,12},{10,14},{12,8},{14,10},{16,20},{18,... | collective-permute-start | bytes 5898248 | tf_op jit(solution)/shard_map/ppermute | solution.py:121
  341.7 43.0 %copy-start.21 = (bf16[8,320,768]{2,1,0:T(8,128)(2,1)S(1)}, bf16[8,320,768]{2,1,0:T(8,128)(2,1)}, u32[]{:S(2)}) copy-start(bf16[8,320,768]{2,1,0:T(8,128)(2,1)} %copy-done.20) | copy-start | bytes 11796484
  344.5 42.3 %copy-start.22 = (bf16[4,320,768]{2,1,0:T(8,128)(2,1)}, bf16[4,320,768]{2,1,0:T(8,128)(2,1)S(1)}, u32[]{:S(2)}) copy-start(bf16[4,320,768]{2,1,0:T(8,128)(2,1)S(1)} %fusion.8) | copy-start | bytes 5898244
  345.7 45.7 %collective-permute-start.6 = (bf16[2,320,768]{2,1,0:T(8,128)(2,1)}, bf16[2,320,768]{2,1,0:T(8,128)(2,1)S(1)}, u32[]{:S(2)}, u32[]{:S(2)}) collective-permute-start(bf16[2,320,768]{2,1,0:T(8,128)(2,1)} %dynamic-slice_bitcast_fusion.5), channel_id=1, source_target_pairs={{0,8},{2,10},{4,12},{6,14},{8,0},{10,2},{12,4},{14,6},{16,24},{18,... | collective-permute-start | bytes 2949128 | tf_op jit(solution)/shard_map/ppermute | solution.py:121
  386.8 1.3 copy-start.23
  389.1 33.3 %collective-permute-start.8 = (bf16[2,320,768]{2,1,0:T(8,128)(2,1)}, bf16[2,320,768]{2,1,0:T(8,128)(2,1)}, u32[]{:S(2)}, u32[]{:S(2)}) collective-permute-start(bf16[2,320,768]{2,1,0:T(8,128)(2,1)} %dynamic-slice_bitcast_fusion.4), channel_id=1, source_target_pairs={{0,8},{2,10},{4,12},{6,14},{8,0},{10,2},{12,4},{14,6},{16,24},{18,... | collective-permute-start | bytes 2949128 | tf_op jit(solution)/shard_map/ppermute | solution.py:121
  391.3 31.0 %copy-start.24 = (bf16[4,320,768]{2,1,0:T(8,128)(2,1)S(1)}, bf16[4,320,768]{2,1,0:T(8,128)(2,1)}, u32[]{:S(2)}) copy-start(bf16[4,320,768]{2,1,0:T(8,128)(2,1)} %copy-done.23) | copy-start | bytes 5898244
  391.3 35.9 %copy-start.27 = (s32[16]{0:T(128)S(1)}, s32[16]{0:T(128)}, u32[]{:S(2)}) copy-start(s32[16]{0:T(128)} %param.13) | copy-start | bytes 196
  392.9 30.9 %copy-start.25 = (bf16[2,320,768]{2,1,0:T(8,128)(2,1)}, bf16[2,320,768]{2,1,0:T(8,128)(2,1)S(1)}, u32[]{:S(2)}) copy-start(bf16[2,320,768]{2,1,0:T(8,128)(2,1)S(1)} %fusion.11) | copy-start | bytes 2949124
  393.8 44.0 %collective-permute-start.7 = (bf16[1,320,768]{2,1,0:T(8,128)(2,1)}, bf16[1,320,768]{2,1,0:T(8,128)(2,1)}, u32[]{:S(2)}, u32[]{:S(2)}) collective-permute-start(bf16[1,320,768]{2,1,0:T(8,128)(2,1)} %constant_dynamic-slice_fusion.1), channel_id=1, source_target_pairs={{0,16},{2,18},{4,20},{6,22},{8,24},{10,26},{12,28},{14,30},{16,0},... | collective-permute-start | bytes 1474568 | tf_op jit(solution)/shard_map/ppermute | solution.py:121
  424.6 22.5 %collective-permute-start.9 = (bf16[1,320,768]{2,1,0:T(8,128)(2,1)}, bf16[1,320,768]{2,1,0:T(8,128)(2,1)}, u32[]{:S(2)}, u32[]{:S(2)}) collective-permute-start(bf16[1,320,768]{2,1,0:T(8,128)(2,1)} %constant_dynamic-slice_fusion), channel_id=1, source_target_pairs={{0,16},{2,18},{4,20},{6,22},{8,24},{10,26},{12,28},{14,30},{16,0},... | collective-permute-start | bytes 1474568 | tf_op jit(solution)/shard_map/ppermute | solution.py:121
  427.9 1.7 copy-start.5
  429.5 1.7 copy-start.8
  431.2 1.7 copy-start.10
  432.9 5.0 %copy-start.26 = (bf16[2,320,768]{2,1,0:T(8,128)(2,1)S(1)}, bf16[2,320,768]{2,1,0:T(8,128)(2,1)}, u32[]{:S(2)}) copy-start(bf16[2,320,768]{2,1,0:T(8,128)(2,1)} %copy-done.25) | copy-start | bytes 2949124
  432.9 6.1 %copy-start.3 = (bf16[3,512,768]{2,1,0:T(8,128)(2,1)S(1)}, bf16[3,512,768]{2,1,0:T(8,128)(2,1)}, u32[]{:S(2)}) copy-start(bf16[3,512,768]{2,1,0:T(8,128)(2,1)} %copy-done.2) | copy-start | bytes 7077892
  439.0 10.8 %copy-start.1 = (s32[16,8]{0,1:T(8,128)S(1)}, s32[16,8]{0,1:T(8,128)}, u32[]{:S(2)}) copy-start(s32[16,8]{0,1:T(8,128)} %param.12) | copy-start | bytes 1540
Sparse Core Ops, SparseCore 0:
  9.6 24.2 all-gather.1
